TPU v7x, 32 devices: a whole 2x2x4 slice. The times are simulated.
32 devices in a mesh: ctx: 8 (over z, x), zero: 4 (over y, core).
Axes of the slice: x: 2, y: 2, z: 4, core: 2. Of those that a mesh axis runs over, the one named last changes fastest.
Arguments:
- activations: bfloat16 [4096, 4096], P('ctx', 'zero'), may hold values from -1200 to 1200
- norm_gain: bfloat16 [4096], replicated, may hold values from 0.099609375 to 1.8984375
- query_weight: bfloat16 [4096, 1024], P('ctx', 'zero'), may hold values from -24 to 24
- kv_weight: bfloat16 [4096, 4, 128], P('ctx', 'zero'), may hold values from -1 to 1
- out_weight: bfloat16 [1024, 4096], P('zero', 'ctx'), may hold values from -0.1875 to 0.1875
- tile_mask: int32 [8, 4, 4], P('ctx'), may hold values from 0 to 1, as said below
- anchor_mask: int32 [8, 4, 4], P('ctx'), may hold values 0 or 1
- anchor_index: int32 [1], replicated, may hold values from 0 to 7
Outputs:
- mixed: bfloat16 [4096, 4096], P(('ctx', 'zero'))
Inputs may be any that keep to these rules, and one draw needn't show every extreme that they name: `tile_mask`: entries of every block's table above the diagonal are 0 and diagonal entries are 1.
All inputs are finite; a program needn't handle non-finite values. No bound on the sum of `anchor_mask` on one device may be relied on, other than what follows from the above.
Results may differ from a plain program's by a relative error of at most 0.02.
Values may be sent and summed in bfloat16 or wider, within the bound.
No kernel may reach another device: no remote copies, remote signals or barrier semaphores. Data moves between devices by JAX's collectives and lax.ppermute only.
A program may use at most 64 MiB of HBM per device.

v0:
```python
import functools
import math

import jax
import jax.numpy as jnp
from jax import lax
from jax.experimental import pallas as pl
from jax.experimental.pallas import tpu as pltpu
from jax.sharding import PartitionSpec as P

HBM = pl.BlockSpec(memory_space=pltpu.HBM)
VMEM = pl.BlockSpec(memory_space=pltpu.VMEM)
SMEM = pl.BlockSpec(memory_space=pltpu.SMEM)
VMEM_LIMIT = 32 * 1024 * 1024
ROPE_BASE = 500000.0


def swap(value, axis, stride):
    pairs = [(source, source ^ stride) for source in range(lax.axis_size(axis))]
    return lax.ppermute(value, axis, pairs)


def cycle(size):
    return list(range(0, size, 2)) + list(range(1, size, 2))[::-1]


def ring_step(value):
    ctx_size, zero_size = lax.axis_size("ctx"), lax.axis_size("zero")
    order = cycle(ctx_size)
    pairs = []
    for at in range(ctx_size):
        for zero in range(zero_size):
            to = order[(at + (1 if zero % 2 == 0 else -1)) % ctx_size]
            pairs.append((order[at] * zero_size + zero, to * zero_size + zero))
    return lax.ppermute(value, ("ctx", "zero"), pairs)


class Ring:
    def __init__(self, shard, core, whole=None, base=0):
        self.held = [(0, None, 0, shard if whole is None else whole)] if base == 0 else []
        self.base = base
        self.moving, self.core, self.at = shard, core, 0
        self.length = lax.axis_size("ctx") // 2

    def step(self, *after):
        self.at += 1
        last = self.at == self.length
        if last:
            half = self.moving.shape[0] // 2
            self.moving = lax.dynamic_slice_in_dim(self.moving, self.core * half, half, 0)
        behind = self.held[-3][3:] if len(self.held) > 3 else []
        self.moving = ring_step(tied(self.moving, *behind, *after))
        self.held.append((-self.at, 0 if last else None, self.base, self.moving))
        self.held.append(
            (self.at, 1 if last else None, self.base, swap(self.moving, "zero", 1))
        )
        return self.moving

    def advance(self, part, parts, *after):
        while self.at < self.length * (part + 1) // parts:
            self.step(*after)
        return self.moving


def tied(value, *others):
    return lax.optimization_barrier((value, *others))[0] if others else value


def source_of(steps):
    size = lax.axis_size("ctx")
    ctx, core = lax.axis_index("ctx"), lax.axis_index("zero") % 2
    place = jnp.where(ctx % 2 == 0, ctx // 2, size - 1 - ctx // 2)
    place = lax.rem(place + steps * (1 - 2 * core) + size, size)
    return jnp.where(place < size // 2, 2 * place, 2 * (size - 1 - place) + 1)


def share_of(share):
    core = lax.axis_index("zero") % 2
    return core if share == 0 else 1 - core


def token_rows(group, other, size):
    core = lax.axis_index("zero") % 2
    if other:
        core = 1 - core
    return pl.ds(pl.multiple_of((2 * group + core) * size, 16), size)


def deal_kernel(count, *refs):
    x_refs, outs, sem = refs[:count], refs[count:-1], refs[-1]
    groups = lax.axis_size("zero") // 2
    size = x_refs[0].shape[0] // (2 * groups)
    copies = []
    for x_ref, out_ref in zip(x_refs, outs):
        for group in range(groups):
            copies.append(
                pltpu.make_async_copy(
                    x_ref.at[token_rows(group, True, size)],
                    out_ref.at[pl.ds(group * size, size)],
                    sem.at[len(copies)],
                )
            )
    for copy in copies:
        copy.start()
    for copy in copies:
        copy.wait()


def deal(arrays):
    tokens, depth = arrays[0].shape
    part = jax.ShapeDtypeStruct((tokens // 2, depth), arrays[0].dtype)
    copies = len(arrays) * lax.axis_size("zero") // 2
    return pl.pallas_call(
        functools.partial(deal_kernel, len(arrays)),
        out_shape=[part] * len(arrays),
        in_specs=[HBM] * len(arrays),
        out_specs=[HBM] * len(arrays),
        scratch_shapes=[pltpu.SemaphoreType.DMA((copies,))],
        compiler_params=pltpu.CompilerParams(vmem_limit_bytes=VMEM_LIMIT),
    )(*arrays)


def project_kernel(layout, *refs):
    (kv_ref, q_ref, x_buf, w_buf, x_sem, w_sem) = refs[-6:]
    pieces, tokens, depth = x_buf.shape
    cos_ref, sin_ref = refs[:2]
    x_refs = refs[2 : 2 + pieces]
    w_refs = refs[2 + pieces : -6]
    zero = lax.axis_index("zero")
    shard_rows = w_refs[0].shape[0]
    x_copies, w_copies = [], []
    for m, ref in enumerate(x_refs):
        target = x_buf.at[jnp.bitwise_xor(zero, m)]
        if m % 2:
            x_copies.append(pltpu.make_async_copy(ref, target, x_sem.at[len(x_copies)]))
            continue
        size = 2 * tokens // pieces
        for group in range(pieces // 2):
            x_copies.append(
                pltpu.make_async_copy(
                    ref.at[token_rows(group, False, size)],
                    target.at[pl.ds(group * size, size)],
                    x_sem.at[len(x_copies)],
                )
            )
    for at, (ref, (steps, share, base)) in enumerate(zip(w_refs, layout)):
        start = source_of(steps) * shard_rows + base
        if share is not None:
            start = start + share_of(share) * ref.shape[0]
        rows = pl.ds(pl.multiple_of(start, 16), ref.shape[0])
        w_copies.append(pltpu.make_async_copy(ref, w_buf.at[rows], w_sem.at[at]))
    for copy in x_copies + w_copies:
        copy.start()
    for copy in x_copies:
        copy.wait()
    squares = jnp.zeros((tokens, 128), jnp.float32)
    for at in range(pieces):
        for first in range(0, depth, 128):
            x_float = x_buf[at, :, first : first + 128].astype(jnp.float32)
            squares += x_float * x_float
    mean = jnp.sum(squares, axis=1, keepdims=True) / (depth * pieces)
    scale = jnp.broadcast_to(lax.rsqrt(mean + 1e-05), squares.shape)
    for copy in w_copies:
        copy.wait()
    head = cos_ref.shape[1]
    shrink = jnp.float32(head ** (-0.5))
    for out_ref, columns in ((kv_ref, 0), (q_ref, 2 * head)):
        for first in range(0, out_ref.shape[1], 2 * head):
            both = slice(columns + first, columns + first + 2 * head)
            total = jnp.zeros((tokens, 2 * head), jnp.float32)
            for at in range(pieces):
                total += jnp.dot(
                    x_buf[at],
                    w_buf[at * depth : (at + 1) * depth, both],
                    preferred_element_type=jnp.float32,
                )
            for at in range(2):
                part = total[:, at * head : (at + 1) * head] * scale
                if columns or not at:
                    part = part * cos_ref[...] + pltpu.roll(part, head // 2, 1) * sin_ref[...]
                if columns:
                    part = part * shrink
                out_ref[:, first + at * head : first + (at + 1) * head] = part.astype(
                    out_ref.dtype
                )


def project(cos, sin, x_pieces, held):
    layout = [(steps, share, base) for steps, share, base, _ in held]
    shards = [piece for _, _, _, piece in held]
    tokens, depth = x_pieces[1].shape
    pieces, head = len(x_pieces), cos.shape[1]
    width = shards[0].shape[1]
    full = depth * pieces
    return pl.pallas_call(
        functools.partial(project_kernel, layout),
        out_shape=[
            jax.ShapeDtypeStruct((tokens, 2 * head), jnp.bfloat16),
            jax.ShapeDtypeStruct((tokens, width - 2 * head), jnp.bfloat16),
        ],
        in_specs=[VMEM] * 2 + [HBM] * (pieces + len(shards)),
        out_specs=[VMEM] * 2,
        scratch_shapes=[
            pltpu.VMEM((pieces, tokens, depth), jnp.bfloat16),
            pltpu.VMEM((full, width), jnp.bfloat16),
            pltpu.SemaphoreType.DMA((pieces // 2 * (1 + pieces // 2),)),
            pltpu.SemaphoreType.DMA((len(shards),)),
        ],
        compiler_params=pltpu.CompilerParams(vmem_limit_bytes=VMEM_LIMIT),
        cost_estimate=pl.CostEstimate(
            flops=2 * tokens * full * width,
            bytes_accessed=2 * full * (tokens + width),
            transcendentals=0,
        ),
    )(cos, sin, *x_pieces, *shards)


def attend_kernel(groups, own_ref, far_ref, *refs):
    keep, send, q_ref, near0, near1, far0, far1, sem = refs[5:]
    copies = [
        pltpu.make_async_copy(source, target, sem.at[at])
        for at, (source, target) in enumerate(zip(refs[:5], refs[7:12]))
    ]
    for copy in copies:
        copy.start()
    for copy in copies:
        copy.wait()
    tokens, pair = near0.shape
    head = pair // 2
    size = tokens // groups
    tiles = own_ref.shape[0]
    tile = 2 * tokens // tiles
    heads = q_ref.shape[1] // head
    rows = heads * size
    core = lax.axis_index("zero") % 2
    column = lax.broadcasted_iota(jnp.int32, (1, tokens), 1)
    column_group = column // size
    within = lax.rem(lax.broadcasted_iota(jnp.int32, (rows, 1), 0), size)
    hidden = jnp.float32(-1e30)
    nt = (((1,), (1,)), ((), ()))
    side = lax.axis_index("zero") // 2 % 2
    for h in range(groups):
        across = slice(h * size, (h + 1) * size)
        q = jnp.concatenate(
            [q_ref[across, g * head : (g + 1) * head] for g in range(heads)], axis=0
        )
        first = (2 * h + core) * size
        own_tile = first // tile
        seen = min(tokens, -(-(h + 1) * size // 128) * 128)
        parts, blocks = [], []
        for ref, mask_ref, width, parity, causal in (
            (far0, far_ref, tokens, core, False),
            (far1, far_ref, tokens, 1 - core, False),
            (near0, own_ref, seen, core, True),
            (near1, own_ref, seen, 1 - core, True),
        ):
            visible = jnp.zeros((1, width), jnp.int32)
            for g in range(-(-width // size)):
                at = mask_ref[own_tile, (2 * g + parity) * size // tile]
                visible = jnp.where(column_group[:, :width] == g, at, visible)
            visible = visible == 1
            if causal:
                group = column_group[:, :width]
                offset = (2 * group + parity) * size + column[:, :width] - group * size
                visible = visible & (offset <= first + within)
            scores = lax.dot_general(
                q, ref[:width, :head], nt, preferred_element_type=jnp.float32
            )
            parts.append(jnp.where(visible, scores, hidden))
            blocks.append((ref, width))
        scores = jnp.concatenate(parts, axis=1)
        largest = jnp.max(scores, axis=1, keepdims=True)
        weights = jnp.exp(scores - largest)
        total = jnp.sum(weights, axis=1, keepdims=True)
        rounded = weights.astype(jnp.bfloat16)
        mixed = jnp.zeros((rows, head), jnp.float32)
        start = 0
        for ref, width in blocks:
            mixed += jnp.dot(
                rounded[:, start : start + width],
                ref[:width, head:],
                preferred_element_type=jnp.float32,
            )
            start += width
        mixed = (mixed / total).astype(keep.dtype)
        rows_out = slice(h // 2 * size, (h // 2 + 1) * size)

        def store(out_ref, rows_out=rows_out, mixed=mixed):
            for g in range(heads):
                out_ref[rows_out, g * head : (g + 1) * head] = mixed[g * size : (g + 1) * size, :]

        pl.when(side == h % 2)(functools.partial(store, keep))
        pl.when(side != h % 2)(functools.partial(store, send))


def attend(groups, own_mask, far_mask, queries, near, near_other, far, far_other):
    tokens, width = queries.shape
    return pl.pallas_call(
        functools.partial(attend_kernel, groups),
        out_shape=[jax.ShapeDtypeStruct((tokens // 2, width), jnp.bfloat16)] * 2,
        in_specs=[SMEM, SMEM] + [HBM] * 5,
        out_specs=[VMEM] * 2,
        scratch_shapes=[pltpu.VMEM(queries.shape, jnp.bfloat16)]
        + [pltpu.VMEM(near.shape, jnp.bfloat16)] * 4
        + [pltpu.SemaphoreType.DMA((5,))],
        compiler_params=pltpu.CompilerParams(vmem_limit_bytes=VMEM_LIMIT),
        cost_estimate=pl.CostEstimate(
            flops=8 * tokens * tokens * width,
            bytes_accessed=8 * tokens * width,
            transcendentals=8 * tokens * tokens,
        ),
    )(own_mask, far_mask, queries, near, near_other, far, far_other)


def mix_kernel(layout, slots, out_refs, *refs):
    count = len(refs) - len(layout) - out_refs - 2
    a_refs, w_refs = refs[:count], refs[count : count + len(layout)]
    outs = refs[count + len(layout) : -2]
    w_buf, sem = refs[-2:]
    width = w_buf.shape[2]
    half = a_refs[0].shape[1]
    copies = []
    for at, (ref, (slot, side, share)) in enumerate(zip(w_refs, layout)):
        rows = ref.shape[0]
        start = side * half
        if share is not None:
            start = pl.multiple_of(start + share_of(share) * rows, 16)
        copies.append(pltpu.make_async_copy(ref, w_buf.at[slot, pl.ds(start, rows)], sem.at[at]))
    for copy in copies:
        copy.start()
    slot = 0
    for out_ref, sides, number in zip(outs, *slots):
        rows = jnp.concatenate([ref[...] for ref in a_refs[:sides]], axis=1)
        for place in range(number):
            for copy, (its_slot, _, _) in zip(copies, layout):
                if its_slot == slot:
                    copy.wait()
            total = jnp.dot(
                rows, w_buf[slot, : sides * half], preferred_element_type=jnp.float32
            )
            out_ref[:, place * width : (place + 1) * width] = total.astype(out_ref.dtype)
            slot += 1


def mix(rows, blocks, dtypes):
    layout, shards = [], []
    sides = [1 + max(side for side, _, _ in block[0]) for block in blocks]
    slots = [slot for block in blocks for slot in block]
    for at, slot in enumerate(slots):
        for side, share, piece in slot:
            layout.append((at, side, share))
            shards.append(piece)
    tokens, half = rows[0].shape
    width = shards[0].shape[1]
    return pl.pallas_call(
        functools.partial(
            mix_kernel, layout, (sides, [len(block) for block in blocks]), len(blocks)
        ),
        out_shape=[
            jax.ShapeDtypeStruct((tokens, width * len(block)), dtype)
            for block, dtype in zip(blocks, dtypes)
        ],
        in_specs=[VMEM] * len(rows) + [HBM] * len(shards),
        out_specs=[VMEM] * len(blocks),
        scratch_shapes=[
            pltpu.VMEM((len(slots), max(sides) * half, width), jnp.bfloat16),
            pltpu.SemaphoreType.DMA((len(shards),)),
        ],
        compiler_params=pltpu.CompilerParams(vmem_limit_bytes=VMEM_LIMIT),
        cost_estimate=pl.CostEstimate(
            flops=2 * tokens * half * width * len(shards),
            bytes_accessed=6 * half * width * len(shards) + 4 * tokens * width * len(slots),
            transcendentals=0,
        ),
    )(*rows, *shards)


def join_kernel(steps, full_ref, keep_ref, *refs):
    got_refs, out_ref = refs[:-1], refs[-1]
    width = out_ref.shape[1] // len(steps)
    whole = full_ref.shape[1] // width
    got = [
        (ref, first) for ref in got_refs for first in range(0, ref.shape[1], width)
    ]
    for slot, along in enumerate(steps):
        start = pl.multiple_of(source_of(along) * width, 128)
        if slot < whole:
            block = full_ref[:, slot * width : (slot + 1) * width]
        else:
            columns = slice((slot - whole) * width, (slot - whole + 1) * width)
            got_ref, first = got[slot - whole]
            block = keep_ref[:, columns] + got_ref[:, first : first + width].astype(jnp.float32)
        out_ref[:, pl.ds(start, width)] = block.astype(out_ref.dtype)


def join(steps, full, keep, gots, dtype):
    rows = full.shape[0]
    columns = full.shape[1] + keep.shape[1]
    return pl.pallas_call(
        functools.partial(join_kernel, steps),
        out_shape=jax.ShapeDtypeStruct((rows, columns), dtype),
        in_specs=[VMEM] * (2 + len(gots)),
        out_specs=VMEM,
        compiler_params=pltpu.CompilerParams(vmem_limit_bytes=VMEM_LIMIT),
        cost_estimate=pl.CostEstimate(
            flops=rows * columns, bytes_accessed=8 * rows * columns, transcendentals=0
        ),
    )(full, keep, *gots)


def exchange_from(value, root, bit):
    other = swap(value, "ctx", 1 << bit)
    same = ((lax.axis_index("ctx") >> bit) & 1) == ((root >> bit) & 1)
    return jnp.where(same, value, other)


def local(
    activations,
    norm_gain,
    query_weight,
    kv_weight,
    out_weight,
    tile_mask,
    anchor_mask,
    anchor_index,
):
    tokens, depth = activations.shape
    head = kv_weight.shape[2]
    ctx_size, zero_size = lax.axis_size("ctx"), lax.axis_size("zero")
    ctx_rank, zero_rank = lax.axis_index("ctx"), lax.axis_index("zero")
    core = zero_rank % 2
    groups = zero_size // 2
    size = tokens // zero_size

    blocks = {0: activations}
    stride = groups
    while stride > 1:
        for known in range(0, zero_size, 2 * stride):
            blocks[known + stride] = swap(blocks[known], "zero", stride)
        stride //= 2

    shard_rows = kv_weight.shape[0]
    gain = lax.dynamic_slice_in_dim(norm_gain, ctx_rank * shard_rows, shard_rows)
    gain = gain.astype(jnp.float32)[:, None]
    kv_own = kv_weight[:, 0, :]
    kv_other, query_other = swap(kv_own, "zero", 1), swap(query_weight, "zero", 1)
    pair = jnp.where(
        core == 0,
        jnp.concatenate([kv_own, kv_other, query_weight, query_other], 1),
        jnp.concatenate([kv_other, kv_own, query_other, query_weight], 1),
    )
    pair = (pair.astype(jnp.float32) * gain).astype(jnp.bfloat16)
    out_other = swap(out_weight, "zero", 1)
    out_pair = jnp.where(
        core == 0,
        jnp.concatenate([out_weight, out_other], 0),
        jnp.concatenate([out_other, out_weight], 0),
    )
    ring_rows = shard_rows // 2
    rings = [
        Ring(pair[:ring_rows], core, pair),
        Ring(pair[ring_rows:], core, None, ring_rows),
    ]
    out_ring = Ring(out_pair, core)
    for part in range(4):
        for ring in rings:
            ring.advance(part, 4)
    held = rings[0].held + rings[1].held
    beyond = [swap(out_weight, "zero", 2)]
    out_ring.advance(0, 4, *[ring.moving for ring in rings], *beyond)

    far_blocks = [tied(blocks[m], rings[0].moving) for m in range(2, zero_size, 2)]
    x_pieces = []
    for at, theirs in enumerate(deal([blocks[0]]) + deal(far_blocks)):
        x_pieces += [([blocks[0]] + far_blocks)[at], swap(theirs, "zero", 1)]

    half = head // 2
    frequency = jnp.power(
        jnp.float32(ROPE_BASE), -(jnp.arange(half, dtype=jnp.float32) * 2.0 / head)
    )
    local_token = jnp.arange(tokens // 2, dtype=jnp.int32)
    offsets = (2 * (local_token // size) + core) * size + local_token % size
    positions = ctx_rank * tokens + offsets
    angles = positions.astype(jnp.float32)[:, None] * frequency[None, :]
    cos_half, sin_half = jnp.cos(angles), jnp.sin(angles)
    cos = jnp.concatenate([cos_half, cos_half], -1)
    sin = jnp.concatenate([-sin_half, sin_half], -1)

    near, queries = project(cos, sin, x_pieces, held)

    def share():
        for at in range(len(beyond), out_ring.at + 1):
            beyond.append(swap(out_ring.held[2 * at - 1][3], "zero", 2))

    share()
    anchor = anchor_index[0]
    far = tied(near, out_ring.moving)
    for bit in range(int(math.log2(ctx_size))):
        far = exchange_from(far, anchor, bit)
        if bit == 0:
            near_other = swap(near, "zero", 1)
            far = tied(far, near_other)
            out_ring.advance(1, 4, far)
    far_other = swap(far, "zero", 1)
    out_ring.advance(2, 4, far_other, beyond[-1])
    far_mask = jnp.where(ctx_rank != anchor, anchor_mask[0], 0)
    keep, send = attend(
        groups, tile_mask[0], far_mask, queries, near, near_other, far, far_other
    )
    got = swap(send, "zero", 2)
    out_ring.held[-1] = (
        *out_ring.held[-1][:3],
        swap(tied(out_ring.moving, send), "zero", 1),
    )
    cut = ctx_size // 4
    block = [
        [(0, None, piece)]
        for steps, _, _, piece in out_ring.held
        if len(beyond) <= abs(steps) <= cut
    ]
    (terms,) = mix([send], [block], [jnp.bfloat16])
    got_terms = [swap(terms, "zero", 2)]
    out_ring.advance(3, 4, terms)

    steps_of, both_chips, one_chip = [], [], []
    for steps, half_of, _, piece in out_ring.held:
        slots = both_chips if abs(steps) < len(beyond) else one_chip
        if half_of != 1:
            steps_of.append(steps)
            slots.append([])
        slots[-1].append((0, half_of, piece))
        if slots is both_chips:
            if steps <= 0:
                across = swap(beyond[-steps], "zero", 1)
            if steps == 0:
                slots[-1] += [(1, 0, beyond[0]), (1, 1, across)]
            else:
                slots[-1].append((1, half_of, beyond[-steps] if steps < 0 else across))
    for block, early in ((one_chip[cut : 2 * cut], [got]), (one_chip[2 * cut :], got_terms[:1])):
        (terms,) = mix([tied(send, *early)], [block], [jnp.bfloat16])
        got_terms.append(swap(terms, "zero", 2))
    full, kept = mix([keep, got], [both_chips, one_chip], [jnp.float32, jnp.float32])
    if zero_size == 4:
        return join(steps_of, full, kept, got_terms, jnp.bfloat16)
    total = join(steps_of, full, kept, got_terms, jnp.float32)
    stride = zero_size // 2
    while stride > 2:
        rows = total.shape[0] // 2
        bit = (zero_rank // stride) % 2
        stay = lax.dynamic_slice_in_dim(total, bit * rows, rows, 0)
        go = lax.dynamic_slice_in_dim(total, (1 - bit) * rows, rows, 0)
        total = stay + swap(go.astype(jnp.bfloat16), "zero", stride).astype(jnp.float32)
        stride //= 2
    return total.astype(jnp.bfloat16)


def solution(mesh):
    placed = (
        P("ctx", "zero"),
        P(),
        P("ctx", "zero"),
        P("ctx", "zero", None),
        P("zero", "ctx"),
        P("ctx", None, None),
        P("ctx", None, None),
        P(),
    )
    return jax.shard_map(
        local, mesh=mesh, in_specs=placed, out_specs=P(("ctx", "zero"), None), check_vma=False
    )
```

profile of v0, /device:TPU:0, one launch (start us, length us, event | category | flops | bytes accessed | tf_op | source)
XLA Modules:
  0.0 110.4 jit_solution(4991678494700980957)
XLA Ops:
  0.5 0.8 dynamic-slice_convert_fusion
  1.3 0.7 collective-permute-done.2
  2.0 1.4 %multiply_convert_fusion.refs_6_ = bf16[512,768]{1,0:T(8,128)(2,1)S(1)} fusion(bf16[512,256]{1,0:T(8,128)(2,1)S(1)} %collective-permute-done.3, bf16[512,256]{1,0:T(8,128)(2,1)} %param.10, bf16[512,128]{1,0:T(8,128)(2,1)S(1)} %collective-permute-done.2, bf16[512,128]{1,0:T(8,128)(2,1)} %bitcast.11, f32[512]{0:T(512)S(1)} %dynamic-slice_convert_fusion, pred[]{:T(512)S(6)} %eq.17), kind=kLoop, calls=%fused_computation | loop fusion | flops 7864320 | bytes 1574913 | tf_op jit(solution)/shard_map/convert_element_type | solution.py:452
  3.4 3.0 %collective-permute-start.4 = (bf16[256,768]{1,0:T(8,128)(2,1)S(1)}, bf16[256,768]{1,0:T(8,128)(2,1)S(1)}, u32[]{:S(2)}, u32[]{:S(2)}) collective-permute-start(bf16[256,768]{1,0:T(8,128)(2,1)S(1)} %get-tuple-element.46), channel_id=1, source_target_pairs={{0,8},{1,5},{2,10},{3,7},{8,16},{9,1},{10,18},{11,3},{16,24},{17,9... | collective-permute-start | bytes 1179656 | tf_op jit(solution)/shard_map/ppermute | solution.py:35
  6.4 1.6 %collective-permute-start.13 = (bf16[256,768]{1,0:T(8,128)(2,1)S(1)}, bf16[256,768]{1,0:T(8,128)(2,1)S(1)}, u32[]{:S(2)}, u32[]{:S(2)}) collective-permute-start(bf16[256,768]{1,0:T(8,128)(2,1)S(1)} %get-tuple-element.45), channel_id=1, source_target_pairs={{0,8},{1,5},{2,10},{3,7},{8,16},{9,1},{10,18},{11,3},{16,24},{17,9... | collective-permute-start | bytes 1179656 | tf_op jit(solution)/shard_map/ppermute | solution.py:35
  8.0 1.5 %collective-permute-start.1 = (bf16[512,1024]{1,0:T(8,128)(2,1)S(1)}, bf16[512,1024]{1,0:T(8,128)(2,1)S(1)}, u32[]{:S(2)}, u32[]{:S(2)}) collective-permute-start(bf16[512,1024]{1,0:T(8,128)(2,1)S(1)} %copy-done), channel_id=1, source_target_pairs={{0,2},{1,3},{2,0},{3,1},{4,6},{5,7},{6,4},{7,5},{8,10},{9,11},{10,... | collective-permute-start | bytes 3145736 | tf_op jit(solution)/shard_map/ppermute | solution.py:20
  9.5 2.6 %collective-permute-done.4.refs_7_ = bf16[256,768]{1,0:T(8,128)(2,1)S(1)} collective-permute-done((bf16[256,768]{1,0:T(8,128)(2,1)S(1)}, bf16[256,768]{1,0:T(8,128)(2,1)S(1)}, u32[]{:S(2)}, u32[]{:S(2)}) %collective-permute-start.4) | collective-permute-done | bytes 393248 | tf_op jit(solution)/shard_map/ppermute | solution.py:35
  12.1 2.1 %collective-permute-start.5 = (bf16[256,768]{1,0:T(8,128)(2,1)S(1)}, bf16[256,768]{1,0:T(8,128)(2,1)}, u32[]{:S(2)}, u32[]{:S(2)}) collective-permute-start(bf16[256,768]{1,0:T(8,128)(2,1)S(1)} %collective-permute-done.4.refs_7_), channel_id=1, source_target_pairs={{0,8},{1,5},{2,10},{3,7},{8,16},{9,1},{10,18},{11,3},{16,24},{17,9... | collective-permute-start | bytes 1179656 | tf_op jit(solution)/shard_map/ppermute | solution.py:35
  14.2 2.1 %collective-permute-done.13.refs_15_ = bf16[256,768]{1,0:T(8,128)(2,1)S(1)} collective-permute-done((bf16[256,768]{1,0:T(8,128)(2,1)S(1)}, bf16[256,768]{1,0:T(8,128)(2,1)S(1)}, u32[]{:S(2)}, u32[]{:S(2)}) %collective-permute-start.13) | collective-permute-done | bytes 393248 | tf_op jit(solution)/shard_map/ppermute | solution.py:35
  16.3 2.1 %collective-permute-start.15 = (bf16[256,768]{1,0:T(8,128)(2,1)S(1)}, bf16[256,768]{1,0:T(8,128)(2,1)}, u32[]{:S(2)}, u32[]{:S(2)}) collective-permute-start(bf16[256,768]{1,0:T(8,128)(2,1)S(1)} %collective-permute-done.13.refs_15_), channel_id=1, source_target_pairs={{0,8},{1,5},{2,10},{3,7},{8,16},{9,1},{10,18},{11,3},{16,24},{17,9... | collective-permute-start | bytes 1179656 | tf_op jit(solution)/shard_map/ppermute | solution.py:35
  18.4 0.7 copy-done.5
  19.2 1.5 %collective-permute-done.5.refs_9_ = bf16[256,768]{1,0:T(8,128)(2,1)} collective-permute-done((bf16[256,768]{1,0:T(8,128)(2,1)S(1)}, bf16[256,768]{1,0:T(8,128)(2,1)}, u32[]{:S(2)}, u32[]{:S(2)}) %collective-permute-start.5) | collective-permute-done | bytes 393248 | tf_op jit(solution)/shard_map/ppermute | solution.py:35
  20.6 0.8 copy-done.7
  21.4 2.1 %collective-permute-start.7 = (bf16[256,768]{1,0:T(8,128)(2,1)}, bf16[256,768]{1,0:T(8,128)(2,1)}, u32[]{:S(2)}, u32[]{:S(2)}) collective-permute-start(bf16[256,768]{1,0:T(8,128)(2,1)} %collective-permute-done.5.refs_9_), channel_id=1, source_target_pairs={{0,8},{1,5},{2,10},{3,7},{8,16},{9,1},{10,18},{11,3},{16,24},{17,9... | collective-permute-start | bytes 1179656 | tf_op jit(solution)/shard_map/ppermute | solution.py:35
  23.5 0.7 copy-done.9
  24.9 2.1 %collective-permute-start.17 = (bf16[256,768]{1,0:T(8,128)(2,1)}, bf16[256,768]{1,0:T(8,128)(2,1)}, u32[]{:S(2)}, u32[]{:S(2)}) collective-permute-start(bf16[256,768]{1,0:T(8,128)(2,1)} %collective-permute-done.15.refs_17_), channel_id=1, source_target_pairs={{0,8},{1,5},{2,10},{3,7},{8,16},{9,1},{10,18},{11,3},{16,24},{17,9... | collective-permute-start | bytes 1179656 | tf_op jit(solution)/shard_map/ppermute | solution.py:35
  27.0 2.5 %collective-permute-done.7.refs_11_ = bf16[256,768]{1,0:T(8,128)(2,1)} collective-permute-done((bf16[256,768]{1,0:T(8,128)(2,1)}, bf16[256,768]{1,0:T(8,128)(2,1)}, u32[]{:S(2)}, u32[]{:S(2)}) %collective-permute-start.7) | collective-permute-done | bytes 393248 | tf_op jit(solution)/shard_map/ppermute | solution.py:35
  29.5 0.9 constant_dynamic-slice_fusion.2
  30.5 2.2 %collective-permute-start.9 = (bf16[128,768]{1,0:T(8,128)(2,1)S(1)}, bf16[128,768]{1,0:T(8,128)(2,1)S(1)}, u32[]{:S(2)}, u32[]{:S(2)}) collective-permute-start(bf16[128,768]{1,0:T(8,128)(2,1)S(1)} %constant_dynamic-slice_fusion.2), channel_id=1, source_target_pairs={{0,8},{1,5},{2,10},{3,7},{8,16},{9,1},{10,18},{11,3},{16,24},{17,9... | collective-permute-start | bytes 589832 | tf_op jit(solution)/shard_map/ppermute | solution.py:35
  33.3 1.5 %collective-permute-start.23 = (bf16[256,512]{1,0:T(8,128)(2,1)}, bf16[256,512]{1,0:T(8,128)(2,1)S(1)}, u32[]{:S(2)}, u32[]{:S(2)}) collective-permute-start(bf16[256,512]{1,0:T(8,128)(2,1)} %param.12), channel_id=1, source_target_pairs={{0,2},{1,3},{2,0},{3,1},{4,6},{5,7},{6,4},{7,5},{8,10},{9,11},{10,... | collective-permute-start | bytes 786440 | tf_op jit(solution)/shard_map/ppermute | solution.py:20
  34.8 0.9 constant_dynamic-slice_fusion.1
  36.2 2.1 %collective-permute-start.19 = (bf16[128,768]{1,0:T(8,128)(2,1)S(1)}, bf16[128,768]{1,0:T(8,128)(2,1)S(1)}, u32[]{:S(2)}, u32[]{:S(2)}) collective-permute-start(bf16[128,768]{1,0:T(8,128)(2,1)S(1)} %constant_dynamic-slice_fusion.1), channel_id=1, source_target_pairs={{0,8},{1,5},{2,10},{3,7},{8,16},{9,1},{10,18},{11,3},{16,24},{17,9... | collective-permute-start | bytes 589832 | tf_op jit(solution)/shard_map/ppermute | solution.py:35
  38.7 3.1 %collective-permute-done.23.refs_3_ = bf16[256,512]{1,0:T(8,128)(2,1)S(1)} collective-permute-done((bf16[256,512]{1,0:T(8,128)(2,1)}, bf16[256,512]{1,0:T(8,128)(2,1)S(1)}, u32[]{:S(2)}, u32[]{:S(2)}) %collective-permute-start.23) | collective-permute-done | bytes 262176 | tf_op jit(solution)/shard_map/ppermute | solution.py:20
  41.9 2.1 %collective-permute-start.24 = (bf16[512,512]{1,0:T(8,128)(2,1)S(1)}, bf16[512,512]{1,0:T(8,128)(2,1)S(1)}, u32[]{:S(2)}, u32[]{:S(2)}) collective-permute-start(bf16[512,512]{1,0:T(8,128)(2,1)S(1)} %maximum_select_fusion.1.refs_2_), channel_id=1, source_target_pairs={{0,8},{1,5},{2,10},{3,7},{8,16},{9,1},{10,18},{11,3},{16,24},{17,9... | collective-permute-start | bytes 1572872 | tf_op jit(solution)/shard_map/ppermute | solution.py:35
  45.8 5.5 %shard_map.84 = (bf16[256,256]{1,0:T(8,128)(2,1)S(1)}, bf16[256,512]{1,0:T(8,128)(2,1)S(1)}) custom-call(f32[256,128]{1,0:T(8,128)S(1)} %get-tuple-element.50.refs_0_, f32[256,128]{1,0:T(8,128)S(1)} %get-tuple-element.51.refs_1_, bf16[512,1024]{1,0:T(8,128)(2,1)S(1)} %copy-done, bf16[256,1024]{1,0:T(8,128)(2,1)S(1)} %collective-permute-done.refs_3_, ...), custom_call_target="tpu_custom_call" | custom-call | flops 1610612736 | bytes 8388608 | tf_op jit(solution)/shard_map/pallas_call | solution.py:195
  52.0 0.8 copy-done.1
  52.8 1.0 collective-permute-start.25
  54.6 3.9 %collective-permute-done.25 = bf16[256,256]{1,0:T(8,128)(2,1)S(1)} collective-permute-done((bf16[256,256]{1,0:T(8,128)(2,1)S(1)}, bf16[256,256]{1,0:T(8,128)(2,1)S(1)}, u32[]{:S(2)}, u32[]{:S(2)}) %collective-permute-start.25) | collective-permute-done | bytes 131104 | tf_op jit(solution)/shard_map/ppermute | solution.py:20
  58.5 1.6 %collective-permute-start.26 = (bf16[256,256]{1,0:T(8,128)(2,1)S(1)}, bf16[256,256]{1,0:T(8,128)(2,1)S(1)}, u32[]{:S(2)}, u32[]{:S(2)}) collective-permute-start(bf16[256,256]{1,0:T(8,128)(2,1)S(1)} %broadcast_select_fusion), channel_id=1, source_target_pairs={{0,8},{4,12},{8,0},{12,4},{16,24},{20,28},{24,16},{28,20},{1,9},{5... | collective-permute-start | bytes 393224 | tf_op jit(solution)/shard_map/ppermute | solution.py:20
  60.1 1.5 %collective-permute-start.31 = (bf16[512,512]{1,0:T(8,128)(2,1)}, bf16[512,512]{1,0:T(8,128)(2,1)S(1)}, u32[]{:S(2)}, u32[]{:S(2)}) collective-permute-start(bf16[512,512]{1,0:T(8,128)(2,1)} %copy-done.1), channel_id=1, source_target_pairs={{0,2},{1,3},{2,0},{3,1},{4,6},{5,7},{6,4},{7,5},{8,10},{9,11},{10,... | collective-permute-start | bytes 1572872 | tf_op jit(solution)/shard_map/ppermute | solution.py:20
  62.1 1.4 %collective-permute-done.26 = bf16[256,256]{1,0:T(8,128)(2,1)S(1)} collective-permute-done((bf16[256,256]{1,0:T(8,128)(2,1)S(1)}, bf16[256,256]{1,0:T(8,128)(2,1)S(1)}, u32[]{:S(2)}, u32[]{:S(2)}) %collective-permute-start.26) | collective-permute-done | bytes 131104 | tf_op jit(solution)/shard_map/ppermute | solution.py:20
  63.5 2.7 %collective-permute-start.27 = (bf16[256,256]{1,0:T(8,128)(2,1)S(1)}, bf16[256,256]{1,0:T(8,128)(2,1)S(1)}, u32[]{:S(2)}, u32[]{:S(2)}) collective-permute-start(bf16[256,256]{1,0:T(8,128)(2,1)S(1)} %broadcast_select_fusion.1), channel_id=1, source_target_pairs={{0,16},{4,20},{8,24},{12,28},{16,0},{20,4},{24,8},{28,12},{1,17},{... | collective-permute-start | bytes 393224 | tf_op jit(solution)/shard_map/ppermute | solution.py:20
  66.2 6.1 %collective-permute-done.27 = bf16[256,256]{1,0:T(8,128)(2,1)S(1)} collective-permute-done((bf16[256,256]{1,0:T(8,128)(2,1)S(1)}, bf16[256,256]{1,0:T(8,128)(2,1)S(1)}, u32[]{:S(2)}, u32[]{:S(2)}) %collective-permute-start.27) | collective-permute-done | bytes 131104 | tf_op jit(solution)/shard_map/ppermute | solution.py:20
  72.4 4.5 %collective-permute-start.28 = (bf16[256,256]{1,0:T(8,128)(2,1)S(1)}, bf16[256,256]{1,0:T(8,128)(2,1)S(1)}, u32[]{:S(2)}, u32[]{:S(2)}) collective-permute-start(bf16[256,256]{1,0:T(8,128)(2,1)S(1)} %broadcast_select_fusion.2.refs_3_), channel_id=1, source_target_pairs={{0,1},{1,0},{2,3},{3,2},{4,5},{5,4},{6,7},{7,6},{8,9},{9,8},{10,11... | collective-permute-start | bytes 393224 | tf_op jit(solution)/shard_map/ppermute | solution.py:20
  76.9 1.0 collective-permute-done.28.refs_4_
  78.5 0.8 collective-permute-start.36
  79.6 0.9 copy-done.14
  80.5 0.9 copy-done.16
  81.4 3.9 %shard_map.85 = (bf16[128,512]{1,0:T(8,128)(2,1)S(1)}, bf16[128,512]{1,0:T(8,128)(2,1)S(1)}) custom-call(s32[4,4]{1,0:T(4,128)S(1)} %bitcast.9, s32[4,4]{1,0:T(4,128)S(1)} %select_bitcast_fusion.far_ref, bf16[256,512]{1,0:T(8,128)(2,1)S(1)} %copy-done.14, bf16[256,256]{1,0:T(8,128)(2,1)S(1)} %get-tuple-element.33.refs_1_, ...), custom_call_target="tpu_custom_call" | custom-call | flops 268435456 | bytes 1048576 | tf_op jit(solution)/shard_map/pallas_call | solution.py:298
  85.3 2.4 %collective-permute-done.36.refs_11_.refs_1_ = bf16[512,512]{1,0:T(8,128)(2,1)S(1)} collective-permute-done((bf16[512,512]{1,0:T(8,128)(2,1)S(1)}, bf16[512,512]{1,0:T(8,128)(2,1)S(1)}, u32[]{:S(2)}, u32[]{:S(2)}) %collective-permute-start.36) | collective-permute-done | bytes 524320 | tf_op jit(solution)/shard_map/ppermute | solution.py:35
  88.3 0.9 collective-permute-start.38
  90.2 1.6 %collective-permute-start.40 = (bf16[128,1024]{1,0:T(8,128)(2,1)S(1)}, bf16[128,1024]{1,0:T(8,128)(2,1)S(1)}, u32[]{:S(2)}, u32[]{:S(2)}) collective-permute-start(bf16[128,1024]{1,0:T(8,128)(2,1)S(1)} %shard_map.86), channel_id=1, source_target_pairs={{0,2},{1,3},{2,0},{3,1},{4,6},{5,7},{6,4},{7,5},{8,10},{9,11},{10,... | collective-permute-start | bytes 786440 | tf_op jit(solution)/shard_map/ppermute | solution.py:20
  91.8 2.9 %collective-permute-done.38.refs_13_.refs_1_ = bf16[256,512]{1,0:T(8,128)(2,1)S(1)} collective-permute-done((bf16[256,512]{1,0:T(8,128)(2,1)S(1)}, bf16[256,512]{1,0:T(8,128)(2,1)S(1)}, u32[]{:S(2)}, u32[]{:S(2)}) %collective-permute-start.38) | collective-permute-done | bytes 262176 | tf_op jit(solution)/shard_map/ppermute | solution.py:35
  94.7 1.4 %collective-permute-done.29.refs_1_ = bf16[128,512]{1,0:T(8,128)(2,1)S(1)} collective-permute-done((bf16[128,512]{1,0:T(8,128)(2,1)S(1)}, bf16[128,512]{1,0:T(8,128)(2,1)S(1)}, u32[]{:S(2)}, u32[]{:S(2)}) %collective-permute-start.29) | collective-permute-done | bytes 131104 | tf_op jit(solution)/shard_map/ppermute | solution.py:20
  97.2 4.4 %collective-permute-done.40.refs_0_ = bf16[128,1024]{1,0:T(8,128)(2,1)S(1)} collective-permute-done((bf16[128,1024]{1,0:T(8,128)(2,1)S(1)}, bf16[128,1024]{1,0:T(8,128)(2,1)S(1)}, u32[]{:S(2)}, u32[]{:S(2)}) %collective-permute-start.40) | collective-permute-done | bytes 262176 | tf_op jit(solution)/shard_map/ppermute | solution.py:20
  102.5 2.7 %shard_map.87 = (f32[128,1536]{1,0:T(8,128)S(1)}, f32[128,2560]{1,0:T(8,128)S(1)}) custom-call(bf16[128,512]{1,0:T(8,128)(2,1)S(1)} %get-tuple-element.35.refs_0_, bf16[128,512]{1,0:T(8,128)(2,1)S(1)} %collective-permute-done.29.refs_1_, bf16[512,512]{1,0:T(8,128)(2,1)S(1)} %maximum_select_fusion.1.refs_2_, bf16[256,512]{1,0:T(8,128)(2,1)S(1)} %copy-done.12, ...), custom_call_target="tpu_custom_call" | custom-call | flops 872415232 | bytes 22544384 | tf_op jit(solution)/shard_map/pallas_call | solution.py:355
  105.2 4.1 %collective-permute-done.42.refs_2_ = bf16[128,512]{1,0:T(8,128)(2,1)S(1)} collective-permute-done((bf16[128,512]{1,0:T(8,128)(2,1)S(1)}, bf16[128,512]{1,0:T(8,128)(2,1)S(1)}, u32[]{:S(2)}, u32[]{:S(2)}) %collective-permute-start.42) | collective-permute-done | bytes 131104 | tf_op jit(solution)/shard_map/ppermute | solution.py:20
  109.2 1.2 %shard_map.90 = bf16[128,4096]{1,0:T(8,128)(2,1)} custom-call(f32[128,1536]{1,0:T(8,128)S(1)} %get-tuple-element.41.full_ref, f32[128,2560]{1,0:T(8,128)S(1)} %get-tuple-element.42.keep_ref, bf16[128,1024]{1,0:T(8,128)(2,1)S(1)} %collective-permute-done.40.refs_0_, bf16[128,1024]{1,0:T(8,128)(2,1)S(1)} %collective-permute-done.41.refs_1_, ...), custom_call_target="tpu_custom_call" | custom-call | flops 524288 | bytes 4194304 | tf_op jit(solution)/shard_map/pallas_call | solution.py:399
  (102 shorter events, 10.1 us)
Async XLA Ops:
  0.0 2.0 %collective-permute-start.3 = (bf16[512,256]{1,0:T(8,128)(2,1)}, bf16[512,256]{1,0:T(8,128)(2,1)S(1)}, u32[]{:S(2)}, u32[]{:S(2)}) collective-permute-start(bf16[512,256]{1,0:T(8,128)(2,1)} %param.10), channel_id=1, source_target_pairs={{0,1},{1,0},{2,3},{3,2},{4,5},{5,4},{6,7},{7,6},{8,9},{9,8},{10,11... | collective-permute-start | bytes 786440 | tf_op jit(solution)/shard_map/ppermute | solution.py:20
  0.5 1.6 %collective-permute-start.2 = (bf16[512,128]{1,0:T(8,128)(2,1)}, bf16[512,128]{1,0:T(8,128)(2,1)S(1)}, u32[]{:S(2)}, u32[]{:S(2)}) collective-permute-start(bf16[512,128]{1,0:T(8,128)(2,1)} %bitcast.10), channel_id=1, source_target_pairs={{0,1},{1,0},{2,3},{3,2},{4,5},{5,4},{6,7},{7,6},{8,9},{9,8},{10,11... | collective-permute-start | bytes 393224 | tf_op jit(solution)/shard_map/ppermute | solution.py:20
  3.4 8.7 %collective-permute-start.4 = (bf16[256,768]{1,0:T(8,128)(2,1)S(1)}, bf16[256,768]{1,0:T(8,128)(2,1)S(1)}, u32[]{:S(2)}, u32[]{:S(2)}) collective-permute-start(bf16[256,768]{1,0:T(8,128)(2,1)S(1)} %get-tuple-element.46), channel_id=1, source_target_pairs={{0,8},{1,5},{2,10},{3,7},{8,16},{9,1},{10,18},{11,3},{16,24},{17,9... | collective-permute-start | bytes 1179656 | tf_op jit(solution)/shard_map/ppermute | solution.py:35
  6.4 9.9 %collective-permute-start.13 = (bf16[256,768]{1,0:T(8,128)(2,1)S(1)}, bf16[256,768]{1,0:T(8,128)(2,1)S(1)}, u32[]{:S(2)}, u32[]{:S(2)}) collective-permute-start(bf16[256,768]{1,0:T(8,128)(2,1)S(1)} %get-tuple-element.45), channel_id=1, source_target_pairs={{0,8},{1,5},{2,10},{3,7},{8,16},{9,1},{10,18},{11,3},{16,24},{17,9... | collective-permute-start | bytes 1179656 | tf_op jit(solution)/shard_map/ppermute | solution.py:35
  8.0 24.8 %collective-permute-start.1 = (bf16[512,1024]{1,0:T(8,128)(2,1)S(1)}, bf16[512,1024]{1,0:T(8,128)(2,1)S(1)}, u32[]{:S(2)}, u32[]{:S(2)}) collective-permute-start(bf16[512,1024]{1,0:T(8,128)(2,1)S(1)} %copy-done), channel_id=1, source_target_pairs={{0,2},{1,3},{2,0},{3,1},{4,6},{5,7},{6,4},{7,5},{8,10},{9,11},{10,... | collective-permute-start | bytes 3145736 | tf_op jit(solution)/shard_map/ppermute | solution.py:20
  12.1 26.3 %copy-start.3 = (bf16[256,768]{1,0:T(8,128)(2,1)}, bf16[256,768]{1,0:T(8,128)(2,1)S(1)}, u32[]{:S(2)}) copy-start(bf16[256,768]{1,0:T(8,128)(2,1)S(1)} %collective-permute-done.4.refs_7_) | copy-start | bytes 1179652
  12.1 8.5 %collective-permute-start.5 = (bf16[256,768]{1,0:T(8,128)(2,1)S(1)}, bf16[256,768]{1,0:T(8,128)(2,1)}, u32[]{:S(2)}, u32[]{:S(2)}) collective-permute-start(bf16[256,768]{1,0:T(8,128)(2,1)S(1)} %collective-permute-done.4.refs_7_), channel_id=1, source_target_pairs={{0,8},{1,5},{2,10},{3,7},{8,16},{9,1},{10,18},{11,3},{16,24},{17,9... | collective-permute-start | bytes 1179656 | tf_op jit(solution)/shard_map/ppermute | solution.py:35
  14.2 6.4 %collective-permute-start.6 = (bf16[256,768]{1,0:T(8,128)(2,1)S(1)}, bf16[256,768]{1,0:T(8,128)(2,1)S(1)}, u32[]{:S(2)}, u32[]{:S(2)}) collective-permute-start(bf16[256,768]{1,0:T(8,128)(2,1)S(1)} %collective-permute-done.4.refs_7_), channel_id=1, source_target_pairs={{0,1},{1,0},{2,3},{3,2},{4,5},{5,4},{6,7},{7,6},{8,9},{9,8},{10,11... | collective-permute-start | bytes 1179656 | tf_op jit(solution)/shard_map/ppermute | solution.py:20
  16.3 7.2 %collective-permute-start.14 = (bf16[256,768]{1,0:T(8,128)(2,1)S(1)}, bf16[256,768]{1,0:T(8,128)(2,1)S(1)}, u32[]{:S(2)}, u32[]{:S(2)}) collective-permute-start(bf16[256,768]{1,0:T(8,128)(2,1)S(1)} %collective-permute-done.13.refs_15_), channel_id=1, source_target_pairs={{0,1},{1,0},{2,3},{3,2},{4,5},{5,4},{6,7},{7,6},{8,9},{9,8},{10,11... | collective-permute-start | bytes 1179656 | tf_op jit(solution)/shard_map/ppermute | solution.py:20
  16.3 8.5 %collective-permute-start.15 = (bf16[256,768]{1,0:T(8,128)(2,1)S(1)}, bf16[256,768]{1,0:T(8,128)(2,1)}, u32[]{:S(2)}, u32[]{:S(2)}) collective-permute-start(bf16[256,768]{1,0:T(8,128)(2,1)S(1)} %collective-permute-done.13.refs_15_), channel_id=1, source_target_pairs={{0,8},{1,5},{2,10},{3,7},{8,16},{9,1},{10,18},{11,3},{16,24},{17,9... | collective-permute-start | bytes 1179656 | tf_op jit(solution)/shard_map/ppermute | solution.py:35
  21.4 8.1 %collective-permute-start.7 = (bf16[256,768]{1,0:T(8,128)(2,1)}, bf16[256,768]{1,0:T(8,128)(2,1)}, u32[]{:S(2)}, u32[]{:S(2)}) collective-permute-start(bf16[256,768]{1,0:T(8,128)(2,1)} %collective-permute-done.5.refs_9_), channel_id=1, source_target_pairs={{0,8},{1,5},{2,10},{3,7},{8,16},{9,1},{10,18},{11,3},{16,24},{17,9... | collective-permute-start | bytes 1179656 | tf_op jit(solution)/shard_map/ppermute | solution.py:35
  23.5 6.9 %collective-permute-start.8 = (bf16[256,768]{1,0:T(8,128)(2,1)}, bf16[256,768]{1,0:T(8,128)(2,1)}, u32[]{:S(2)}, u32[]{:S(2)}) collective-permute-start(bf16[256,768]{1,0:T(8,128)(2,1)} %collective-permute-done.5.refs_9_), channel_id=1, source_target_pairs={{0,1},{1,0},{2,3},{3,2},{4,5},{5,4},{6,7},{7,6},{8,9},{9,8},{10,11... | collective-permute-start | bytes 1179656 | tf_op jit(solution)/shard_map/ppermute | solution.py:20
  24.9 8.4 %collective-permute-start.16 = (bf16[256,768]{1,0:T(8,128)(2,1)}, bf16[256,768]{1,0:T(8,128)(2,1)}, u32[]{:S(2)}, u32[]{:S(2)}) collective-permute-start(bf16[256,768]{1,0:T(8,128)(2,1)} %collective-permute-done.15.refs_17_), channel_id=1, source_target_pairs={{0,1},{1,0},{2,3},{3,2},{4,5},{5,4},{6,7},{7,6},{8,9},{9,8},{10,11... | collective-permute-start | bytes 1179656 | tf_op jit(solution)/shard_map/ppermute | solution.py:20
  24.9 10.0 %collective-permute-start.17 = (bf16[256,768]{1,0:T(8,128)(2,1)}, bf16[256,768]{1,0:T(8,128)(2,1)}, u32[]{:S(2)}, u32[]{:S(2)}) collective-permute-start(bf16[256,768]{1,0:T(8,128)(2,1)} %collective-permute-done.15.refs_17_), channel_id=1, source_target_pairs={{0,8},{1,5},{2,10},{3,7},{8,16},{9,1},{10,18},{11,3},{16,24},{17,9... | collective-permute-start | bytes 1179656 | tf_op jit(solution)/shard_map/ppermute | solution.py:35
  30.5 5.7 %collective-permute-start.9 = (bf16[128,768]{1,0:T(8,128)(2,1)S(1)}, bf16[128,768]{1,0:T(8,128)(2,1)S(1)}, u32[]{:S(2)}, u32[]{:S(2)}) collective-permute-start(bf16[128,768]{1,0:T(8,128)(2,1)S(1)} %constant_dynamic-slice_fusion.2), channel_id=1, source_target_pairs={{0,8},{1,5},{2,10},{3,7},{8,16},{9,1},{10,18},{11,3},{16,24},{17,9... | collective-permute-start | bytes 589832 | tf_op jit(solution)/shard_map/ppermute | solution.py:35
  32.7 11.3 %collective-permute-start = (bf16[256,1024]{1,0:T(8,128)(2,1)S(1)}, bf16[256,1024]{1,0:T(8,128)(2,1)S(1)}, u32[]{:S(2)}, u32[]{:S(2)}) collective-permute-start(bf16[256,1024]{1,0:T(8,128)(2,1)S(1)} %shard_map.82), channel_id=1, source_target_pairs={{0,1},{1,0},{2,3},{3,2},{4,5},{5,4},{6,7},{7,6},{8,9},{9,8},{10,11... | collective-permute-start | bytes 1572872 | tf_op jit(solution)/shard_map/ppermute | solution.py:20
  32.8 5.6 %collective-permute-start.22 = (bf16[256,512]{1,0:T(8,128)(2,1)}, bf16[256,512]{1,0:T(8,128)(2,1)S(1)}, u32[]{:S(2)}, u32[]{:S(2)}) collective-permute-start(bf16[256,512]{1,0:T(8,128)(2,1)} %param.12), channel_id=1, source_target_pairs={{0,1},{1,0},{2,3},{3,2},{4,5},{5,4},{6,7},{7,6},{8,9},{9,8},{10,11... | collective-permute-start | bytes 786440 | tf_op jit(solution)/shard_map/ppermute | solution.py:20
  33.3 8.5 %collective-permute-start.23 = (bf16[256,512]{1,0:T(8,128)(2,1)}, bf16[256,512]{1,0:T(8,128)(2,1)S(1)}, u32[]{:S(2)}, u32[]{:S(2)}) collective-permute-start(bf16[256,512]{1,0:T(8,128)(2,1)} %param.12), channel_id=1, source_target_pairs={{0,2},{1,3},{2,0},{3,1},{4,6},{5,7},{6,4},{7,5},{8,10},{9,11},{10,... | collective-permute-start | bytes 786440 | tf_op jit(solution)/shard_map/ppermute | solution.py:20
  34.8 9.3 %collective-permute-start.11 = (bf16[256,768]{1,0:T(8,128)(2,1)}, bf16[256,768]{1,0:T(8,128)(2,1)S(1)}, u32[]{:S(2)}, u32[]{:S(2)}) collective-permute-start(bf16[256,768]{1,0:T(8,128)(2,1)} %collective-permute-done.7.refs_11_), channel_id=1, source_target_pairs={{0,1},{1,0},{2,3},{3,2},{4,5},{5,4},{6,7},{7,6},{8,9},{9,8},{10,11... | collective-permute-start | bytes 1179656 | tf_op jit(solution)/shard_map/ppermute | solution.py:20
  36.2 5.7 %collective-permute-start.19 = (bf16[128,768]{1,0:T(8,128)(2,1)S(1)}, bf16[128,768]{1,0:T(8,128)(2,1)S(1)}, u32[]{:S(2)}, u32[]{:S(2)}) collective-permute-start(bf16[128,768]{1,0:T(8,128)(2,1)S(1)} %constant_dynamic-slice_fusion.1), channel_id=1, source_target_pairs={{0,8},{1,5},{2,10},{3,7},{8,16},{9,1},{10,18},{11,3},{16,24},{17,9... | collective-permute-start | bytes 589832 | tf_op jit(solution)/shard_map/ppermute | solution.py:35
  38.4 7.3 %collective-permute-start.10 = (bf16[256,1024]{1,0:T(8,128)(2,1)S(1)}, bf16[256,1024]{1,0:T(8,128)(2,1)S(1)}, u32[]{:S(2)}, u32[]{:S(2)}) collective-permute-start(bf16[256,1024]{1,0:T(8,128)(2,1)S(1)} %shard_map.83), channel_id=1, source_target_pairs={{0,1},{1,0},{2,3},{3,2},{4,5},{5,4},{6,7},{7,6},{8,9},{9,8},{10,11... | collective-permute-start | bytes 1572872 | tf_op jit(solution)/shard_map/ppermute | solution.py:20
  41.8 3.7 %collective-permute-start.18 = (bf16[256,768]{1,0:T(8,128)(2,1)}, bf16[256,768]{1,0:T(8,128)(2,1)S(1)}, u32[]{:S(2)}, u32[]{:S(2)}) collective-permute-start(bf16[256,768]{1,0:T(8,128)(2,1)} %collective-permute-done.17.refs_19_), channel_id=1, source_target_pairs={{0,1},{1,0},{2,3},{3,2},{4,5},{5,4},{6,7},{7,6},{8,9},{9,8},{10,11... | collective-permute-start | bytes 1179656 | tf_op jit(solution)/shard_map/ppermute | solution.py:20
  41.9 10.2 %collective-permute-start.24 = (bf16[512,512]{1,0:T(8,128)(2,1)S(1)}, bf16[512,512]{1,0:T(8,128)(2,1)S(1)}, u32[]{:S(2)}, u32[]{:S(2)}) collective-permute-start(bf16[512,512]{1,0:T(8,128)(2,1)S(1)} %maximum_select_fusion.1.refs_2_), channel_id=1, source_target_pairs={{0,8},{1,5},{2,10},{3,7},{8,16},{9,1},{10,18},{11,3},{16,24},{17,9... | collective-permute-start | bytes 1572872 | tf_op jit(solution)/shard_map/ppermute | solution.py:35
  44.0 1.5 %collective-permute-start.12 = (bf16[128,768]{1,0:T(8,128)(2,1)S(1)}, bf16[128,768]{1,0:T(8,128)(2,1)S(1)}, u32[]{:S(2)}, u32[]{:S(2)}) collective-permute-start(bf16[128,768]{1,0:T(8,128)(2,1)S(1)} %collective-permute-done.9.refs_13_), channel_id=1, source_target_pairs={{0,1},{1,0},{2,3},{3,2},{4,5},{5,4},{6,7},{7,6},{8,9},{9,8},{10,11... | collective-permute-start | bytes 589832 | tf_op jit(solution)/shard_map/ppermute | solution.py:20
  44.1 1.7 %collective-permute-start.20 = (bf16[128,768]{1,0:T(8,128)(2,1)S(1)}, bf16[128,768]{1,0:T(8,128)(2,1)S(1)}, u32[]{:S(2)}, u32[]{:S(2)}) collective-permute-start(bf16[128,768]{1,0:T(8,128)(2,1)S(1)} %collective-permute-done.19.refs_21_), channel_id=1, source_target_pairs={{0,1},{1,0},{2,3},{3,2},{4,5},{5,4},{6,7},{7,6},{8,9},{9,8},{10,11... | collective-permute-start | bytes 589832 | tf_op jit(solution)/shard_map/ppermute | solution.py:20
  45.8 33.8 %copy-start.19 = (s32[1,4,4]{2,1,0:T(4,128)S(1)}, s32[1,4,4]{2,1,0:T(4,128)}, u32[]{:S(2)}) copy-start(s32[1,4,4]{2,1,0:T(4,128)} %param.14) | copy-start | bytes 196
  45.8 33.8 %copy-start.17 = (s32[1,4,4]{2,1,0:T(4,128)S(1)}, s32[1,4,4]{2,1,0:T(4,128)}, u32[]{:S(2)}) copy-start(s32[1,4,4]{2,1,0:T(4,128)} %param.13) | copy-start | bytes 196
  52.8 5.6 %collective-permute-start.25 = (bf16[256,256]{1,0:T(8,128)(2,1)S(1)}, bf16[256,256]{1,0:T(8,128)(2,1)S(1)}, u32[]{:S(2)}, u32[]{:S(2)}) collective-permute-start(bf16[256,256]{1,0:T(8,128)(2,1)S(1)} %get-tuple-element.33.refs_1_), channel_id=1, source_target_pairs={{0,4},{4,0},{8,12},{12,8},{16,20},{20,16},{24,28},{28,24},{1,5},{5... | collective-permute-start | bytes 393224 | tf_op jit(solution)/shard_map/ppermute | solution.py:20
  54.5 4.0 %collective-permute-start.21 = (bf16[256,256]{1,0:T(8,128)(2,1)S(1)}, bf16[256,256]{1,0:T(8,128)(2,1)S(1)}, u32[]{:S(2)}, u32[]{:S(2)}) collective-permute-start(bf16[256,256]{1,0:T(8,128)(2,1)S(1)} %get-tuple-element.33.refs_1_), channel_id=1, source_target_pairs={{0,1},{1,0},{2,3},{3,2},{4,5},{5,4},{6,7},{7,6},{8,9},{9,8},{10,11... | collective-permute-start | bytes 393224 | tf_op jit(solution)/shard_map/ppermute | solution.py:20
  58.5 5.0 %collective-permute-start.26 = (bf16[256,256]{1,0:T(8,128)(2,1)S(1)}, bf16[256,256]{1,0:T(8,128)(2,1)S(1)}, u32[]{:S(2)}, u32[]{:S(2)}) collective-permute-start(bf16[256,256]{1,0:T(8,128)(2,1)S(1)} %broadcast_select_fusion), channel_id=1, source_target_pairs={{0,8},{4,12},{8,0},{12,4},{16,24},{20,28},{24,16},{28,20},{1,9},{5... | collective-permute-start | bytes 393224 | tf_op jit(solution)/shard_map/ppermute | solution.py:20
  60.1 16.7 %collective-permute-start.31 = (bf16[512,512]{1,0:T(8,128)(2,1)}, bf16[512,512]{1,0:T(8,128)(2,1)S(1)}, u32[]{:S(2)}, u32[]{:S(2)}) collective-permute-start(bf16[512,512]{1,0:T(8,128)(2,1)} %copy-done.1), channel_id=1, source_target_pairs={{0,2},{1,3},{2,0},{3,1},{4,6},{5,7},{6,4},{7,5},{8,10},{9,11},{10,... | collective-permute-start | bytes 1572872 | tf_op jit(solution)/shard_map/ppermute | solution.py:20
  61.6 15.2 %collective-permute-start.32 = (bf16[512,512]{1,0:T(8,128)(2,1)}, bf16[512,512]{1,0:T(8,128)(2,1)S(1)}, u32[]{:S(2)}, u32[]{:S(2)}) collective-permute-start(bf16[512,512]{1,0:T(8,128)(2,1)} %copy-done.1), channel_id=1, source_target_pairs={{0,1},{1,0},{2,3},{3,2},{4,5},{5,4},{6,7},{7,6},{8,9},{9,8},{10,11... | collective-permute-start | bytes 1572872 | tf_op jit(solution)/shard_map/ppermute | solution.py:20
  61.7 16.9 %collective-permute-start.34 = (bf16[512,512]{1,0:T(8,128)(2,1)}, bf16[512,512]{1,0:T(8,128)(2,1)S(1)}, u32[]{:S(2)}, u32[]{:S(2)}) collective-permute-start(bf16[512,512]{1,0:T(8,128)(2,1)} %copy-done.1), channel_id=1, source_target_pairs={{0,8},{1,5},{2,10},{3,7},{8,16},{9,1},{10,18},{11,3},{16,24},{17,9... | collective-permute-start | bytes 1572872 | tf_op jit(solution)/shard_map/ppermute | solution.py:35
  63.5 8.8 %collective-permute-start.27 = (bf16[256,256]{1,0:T(8,128)(2,1)S(1)}, bf16[256,256]{1,0:T(8,128)(2,1)S(1)}, u32[]{:S(2)}, u32[]{:S(2)}) collective-permute-start(bf16[256,256]{1,0:T(8,128)(2,1)S(1)} %broadcast_select_fusion.1), channel_id=1, source_target_pairs={{0,16},{4,20},{8,24},{12,28},{16,0},{20,4},{24,8},{28,12},{1,17},{... | collective-permute-start | bytes 393224 | tf_op jit(solution)/shard_map/ppermute | solution.py:20
  72.4 5.5 %collective-permute-start.28 = (bf16[256,256]{1,0:T(8,128)(2,1)S(1)}, bf16[256,256]{1,0:T(8,128)(2,1)S(1)}, u32[]{:S(2)}, u32[]{:S(2)}) collective-permute-start(bf16[256,256]{1,0:T(8,128)(2,1)S(1)} %broadcast_select_fusion.2.refs_3_), channel_id=1, source_target_pairs={{0,1},{1,0},{2,3},{3,2},{4,5},{5,4},{6,7},{7,6},{8,9},{9,8},{10,11... | collective-permute-start | bytes 393224 | tf_op jit(solution)/shard_map/ppermute | solution.py:20
  78.5 9.2 %collective-permute-start.36 = (bf16[512,512]{1,0:T(8,128)(2,1)S(1)}, bf16[512,512]{1,0:T(8,128)(2,1)S(1)}, u32[]{:S(2)}, u32[]{:S(2)}) collective-permute-start(bf16[512,512]{1,0:T(8,128)(2,1)S(1)} %collective-permute-done.34.refs_1_.refs_9_), channel_id=1, source_target_pairs={{0,8},{1,5},{2,10},{3,7},{8,16},{9,1},{10,18},{11,3},{16,24},{17,9... | collective-permute-start | bytes 1572872 | tf_op jit(solution)/shard_map/ppermute | solution.py:35
  79.3 8.4 %collective-permute-start.35 = (bf16[512,512]{1,0:T(8,128)(2,1)S(1)}, bf16[512,512]{1,0:T(8,128)(2,1)S(1)}, u32[]{:S(2)}, u32[]{:S(2)}) collective-permute-start(bf16[512,512]{1,0:T(8,128)(2,1)S(1)} %collective-permute-done.34.refs_1_.refs_9_), channel_id=1, source_target_pairs={{0,1},{1,0},{2,3},{3,2},{4,5},{5,4},{6,7},{7,6},{8,9},{9,8},{10,11... | collective-permute-start | bytes 1572872 | tf_op jit(solution)/shard_map/ppermute | solution.py:20
  81.4 14.7 %copy-start.12 = (bf16[256,512]{1,0:T(8,128)(2,1)S(1)}, bf16[256,512]{1,0:T(8,128)(2,1)}, u32[]{:S(2)}) copy-start(bf16[256,512]{1,0:T(8,128)(2,1)} %copy-done.11) | copy-start | bytes 786436
  87.7 8.5 %collective-permute-start.37 = (bf16[512,512]{1,0:T(8,128)(2,1)S(1)}, bf16[512,512]{1,0:T(8,128)(2,1)S(1)}, u32[]{:S(2)}, u32[]{:S(2)}) collective-permute-start(bf16[512,512]{1,0:T(8,128)(2,1)S(1)} %collective-permute-done.36.refs_11_.refs_1_), channel_id=1, source_target_pairs={{0,1},{1,0},{2,3},{3,2},{4,5},{5,4},{6,7},{7,6},{8,9},{9,8},{10,11... | collective-permute-start | bytes 1572872 | tf_op jit(solution)/shard_map/ppermute | solution.py:20
  88.3 14.2 %copy-start.2 = (bf16[512,512]{1,0:T(8,128)(2,1)S(1)}, bf16[512,512]{1,0:T(8,128)(2,1)}, u32[]{:S(2)}) copy-start(bf16[512,512]{1,0:T(8,128)(2,1)} %copy-done.1) | copy-start | bytes 1572868
  88.3 6.4 %collective-permute-start.38 = (bf16[256,512]{1,0:T(8,128)(2,1)S(1)}, bf16[256,512]{1,0:T(8,128)(2,1)S(1)}, u32[]{:S(2)}, u32[]{:S(2)}) collective-permute-start(bf16[256,512]{1,0:T(8,128)(2,1)S(1)} %constant_dynamic-slice_fusion), channel_id=1, source_target_pairs={{0,8},{1,5},{2,10},{3,7},{8,16},{9,1},{10,18},{11,3},{16,24},{17,9... | collective-permute-start | bytes 786440 | tf_op jit(solution)/shard_map/ppermute | solution.py:35
  89.2 13.3 %collective-permute-start.33 = (bf16[512,512]{1,0:T(8,128)(2,1)S(1)}, bf16[512,512]{1,0:T(8,128)(2,1)S(1)}, u32[]{:S(2)}, u32[]{:S(2)}) collective-permute-start(bf16[512,512]{1,0:T(8,128)(2,1)S(1)} %collective-permute-done.31.refs_6_), channel_id=1, source_target_pairs={{0,1},{1,0},{2,3},{3,2},{4,5},{5,4},{6,7},{7,6},{8,9},{9,8},{10,11... | collective-permute-start | bytes 1572872 | tf_op jit(solution)/shard_map/ppermute | solution.py:20
  89.8 6.4 %collective-permute-start.29 = (bf16[128,512]{1,0:T(8,128)(2,1)S(1)}, bf16[128,512]{1,0:T(8,128)(2,1)S(1)}, u32[]{:S(2)}, u32[]{:S(2)}) collective-permute-start(bf16[128,512]{1,0:T(8,128)(2,1)S(1)} %get-tuple-element.44.refs_0_), channel_id=1, source_target_pairs={{0,2},{1,3},{2,0},{3,1},{4,6},{5,7},{6,4},{7,5},{8,10},{9,11},{10,... | collective-permute-start | bytes 393224 | tf_op jit(solution)/shard_map/ppermute | solution.py:20
  90.2 11.4 %collective-permute-start.40 = (bf16[128,1024]{1,0:T(8,128)(2,1)S(1)}, bf16[128,1024]{1,0:T(8,128)(2,1)S(1)}, u32[]{:S(2)}, u32[]{:S(2)}) collective-permute-start(bf16[128,1024]{1,0:T(8,128)(2,1)S(1)} %shard_map.86), channel_id=1, source_target_pairs={{0,2},{1,3},{2,0},{3,1},{4,6},{5,7},{6,4},{7,5},{8,10},{9,11},{10,... | collective-permute-start | bytes 786440 | tf_op jit(solution)/shard_map/ppermute | solution.py:20
  94.7 6.9 %collective-permute-start.39 = (bf16[256,512]{1,0:T(8,128)(2,1)S(1)}, bf16[256,512]{1,0:T(8,128)(2,1)S(1)}, u32[]{:S(2)}, u32[]{:S(2)}) collective-permute-start(bf16[256,512]{1,0:T(8,128)(2,1)S(1)} %collective-permute-done.38.refs_13_.refs_1_), channel_id=1, source_target_pairs={{0,1},{1,0},{2,3},{3,2},{4,5},{5,4},{6,7},{7,6},{8,9},{9,8},{10,11... | collective-permute-start | bytes 786440 | tf_op jit(solution)/shard_map/ppermute | solution.py:20
  96.1 6.3 %collective-permute-start.30 = (bf16[256,512]{1,0:T(8,128)(2,1)S(1)}, bf16[256,512]{1,0:T(8,128)(2,1)S(1)}, u32[]{:S(2)}, u32[]{:S(2)}) collective-permute-start(bf16[256,512]{1,0:T(8,128)(2,1)S(1)} %copy-done.12), channel_id=1, source_target_pairs={{0,1},{1,0},{2,3},{3,2},{4,5},{5,4},{6,7},{7,6},{8,9},{9,8},{10,11... | collective-permute-start | bytes 786440 | tf_op jit(solution)/shard_map/ppermute | solution.py:20
  96.7 12.5 %collective-permute-start.41 = (bf16[128,1024]{1,0:T(8,128)(2,1)S(1)}, bf16[128,1024]{1,0:T(8,128)(2,1)S(1)}, u32[]{:S(2)}, u32[]{:S(2)}) collective-permute-start(bf16[128,1024]{1,0:T(8,128)(2,1)S(1)} %shard_map.88), channel_id=1, source_target_pairs={{0,2},{1,3},{2,0},{3,1},{4,6},{5,7},{6,4},{7,5},{8,10},{9,11},{10,... | collective-permute-start | bytes 786440 | tf_op jit(solution)/shard_map/ppermute | solution.py:20
  101.9 7.3 %collective-permute-start.42 = (bf16[128,512]{1,0:T(8,128)(2,1)S(1)}, bf16[128,512]{1,0:T(8,128)(2,1)S(1)}, u32[]{:S(2)}, u32[]{:S(2)}) collective-permute-start(bf16[128,512]{1,0:T(8,128)(2,1)S(1)} %shard_map.89), channel_id=1, source_target_pairs={{0,2},{1,3},{2,0},{3,1},{4,6},{5,7},{6,4},{7,5},{8,10},{9,11},{10,... | collective-permute-start | bytes 393224 | tf_op jit(solution)/shard_map/ppermute | solution.py:20
  (15 other events, 51.7 us)
where the time goes:
time: 111 us; the launch traced here: 110 us
  waiting for transfers between devices  41.8 us (38%)
  starting transfers between devices  41.5 us (37%)
  Pallas kernels  14.7 us (13%)
  local copies, waits for them, and re-layouts  8.26 us (7%)
  other arithmetic  3.06 us (3%)
    ppermute x31, waiting for transfers between devices, swap(): return lax.ppermute(value, axis, pairs)  26.6 us
    ppermute x12, starting transfers between devices, ring_step(): return lax.ppermute(value, ('ctx', 'zero'), pairs)  21.5 us
    ppermute x31, starting transfers between devices, swap(): return lax.ppermute(value, axis, pairs)  20 us
    ppermute x12, waiting for transfers between devices, ring_step(): return lax.ppermute(value, ('ctx', 'zero'), pairs)  15.1 us
    unnamed x40, local copies, waits for them, and re-layouts  6.3 us
    pallas_call x1, Pallas kernels, project(): pl.pallas_call(functools.partial(project_kernel, layout), out_shape=[jax....  5.49 us
    pallas_call x4, Pallas kernels, mix(): pl.pallas_call(functools.partial(mix_kernel, layout, (sides, [len(block)...  4.1 us
    pallas_call x1, Pallas kernels, attend(): pl.pallas_call(functools.partial(attend_kernel, groups), out_shape=[jax.S...  3.85 us
  transfers between devices with their start and end apart: 43, of which 20 were waited for; matrix products, arithmetic and copies ran while one was open for 3% of the time, Pallas kernels for 12%

commit v1 on v0

--- a/solution.py
+++ b/solution.py
@@ -312,7 +312,7 @@
     )(own_mask, far_mask, queries, near, near_other, far, far_other)
 
 
-def mix_kernel(layout, slots, out_refs, *refs):
+def mix_kernel(layout, slots, out_refs, carry, *refs):
     count = len(refs) - len(layout) - out_refs - 2
     a_refs, w_refs = refs[:count], refs[count : count + len(layout)]
     outs = refs[count + len(layout) : -2]
@@ -330,7 +330,9 @@
         copy.start()
     slot = 0
     for out_ref, sides, number in zip(outs, *slots):
-        rows = jnp.concatenate([ref[...] for ref in a_refs[:sides]], axis=1)
+        rows = jnp.concatenate([ref[:, :half] for ref in a_refs[:sides]], axis=1)
+        if carry:
+            out_ref[:, :half] = rows
         for place in range(number):
             for copy, (its_slot, _, _) in zip(copies, layout):
                 if its_slot == slot:
@@ -338,11 +340,12 @@
             total = jnp.dot(
                 rows, w_buf[slot, : sides * half], preferred_element_type=jnp.float32
             )
-            out_ref[:, place * width : (place + 1) * width] = total.astype(out_ref.dtype)
+            start = place * width + (half if carry else 0)
+            out_ref[:, start : start + width] = total.astype(out_ref.dtype)
             slot += 1
 
 
-def mix(rows, blocks, dtypes):
+def mix(rows, blocks, dtypes, carry=False):
     layout, shards = [], []
     sides = [1 + max(side for side, _, _ in block[0]) for block in blocks]
     slots = [slot for block in blocks for slot in block]
@@ -354,10 +357,10 @@
     width = shards[0].shape[1]
     return pl.pallas_call(
         functools.partial(
-            mix_kernel, layout, (sides, [len(block) for block in blocks]), len(blocks)
+            mix_kernel, layout, (sides, [len(block) for block in blocks]), len(blocks), carry
         ),
         out_shape=[
-            jax.ShapeDtypeStruct((tokens, width * len(block)), dtype)
+            jax.ShapeDtypeStruct((tokens, width * len(block) + (half if carry else 0)), dtype)
             for block, dtype in zip(blocks, dtypes)
         ],
         in_specs=[VMEM] * len(rows) + [HBM] * len(shards),
@@ -375,12 +378,14 @@
     )(*rows, *shards)
 
 
-def join_kernel(steps, full_ref, keep_ref, *refs):
+def join_kernel(steps, carried, full_ref, keep_ref, *refs):
     got_refs, out_ref = refs[:-1], refs[-1]
     width = out_ref.shape[1] // len(steps)
     whole = full_ref.shape[1] // width
     got = [
-        (ref, first) for ref in got_refs for first in range(0, ref.shape[1], width)
+        (ref, first)
+        for at, ref in enumerate(got_refs)
+        for first in range(0 if at else carried, ref.shape[1], width)
     ]
     for slot, along in enumerate(steps):
         start = pl.multiple_of(source_of(along) * width, 128)
@@ -393,11 +398,11 @@
         out_ref[:, pl.ds(start, width)] = block.astype(out_ref.dtype)
 
 
-def join(steps, full, keep, gots, dtype):
+def join(steps, carried, full, keep, gots, dtype):
     rows = full.shape[0]
     columns = full.shape[1] + keep.shape[1]
     return pl.pallas_call(
-        functools.partial(join_kernel, steps),
+        functools.partial(join_kernel, steps, carried),
         out_shape=jax.ShapeDtypeStruct((rows, columns), dtype),
         in_specs=[VMEM] * (2 + len(gots)),
         out_specs=VMEM,
@@ -507,19 +512,19 @@
     keep, send = attend(
         groups, tile_mask[0], far_mask, queries, near, near_other, far, far_other
     )
-    got = swap(send, "zero", 2)
-    out_ring.held[-1] = (
-        *out_ring.held[-1][:3],
-        swap(tied(out_ring.moving, send), "zero", 1),
-    )
     cut = ctx_size // 4
     block = [
         [(0, None, piece)]
         for steps, _, _, piece in out_ring.held
         if len(beyond) <= abs(steps) <= cut
     ]
-    (terms,) = mix([send], [block], [jnp.bfloat16])
-    got_terms = [swap(terms, "zero", 2)]
+    (terms,) = mix([send], [block], [jnp.bfloat16], carry=True)
+    out_ring.held[-1] = (
+        *out_ring.held[-1][:3],
+        swap(tied(out_ring.moving, terms), "zero", 1),
+    )
+    got = swap(terms, "zero", 2)
+    got_terms = [got]
     out_ring.advance(3, 4, terms)
 
     steps_of, both_chips, one_chip = [], [], []
@@ -536,13 +541,13 @@
                 slots[-1] += [(1, 0, beyond[0]), (1, 1, across)]
             else:
                 slots[-1].append((1, half_of, beyond[-steps] if steps < 0 else across))
-    for block, early in ((one_chip[cut : 2 * cut], [got]), (one_chip[2 * cut :], got_terms[:1])):
+    for block, early in ((one_chip[cut : 2 * cut], []), (one_chip[2 * cut :], [got])):
         (terms,) = mix([tied(send, *early)], [block], [jnp.bfloat16])
         got_terms.append(swap(terms, "zero", 2))
     full, kept = mix([keep, got], [both_chips, one_chip], [jnp.float32, jnp.float32])
     if zero_size == 4:
-        return join(steps_of, full, kept, got_terms, jnp.bfloat16)
-    total = join(steps_of, full, kept, got_terms, jnp.float32)
+        return join(steps_of, send.shape[1], full, kept, got_terms, jnp.bfloat16)
+    total = join(steps_of, send.shape[1], full, kept, got_terms, jnp.float32)
     stride = zero_size // 2
     while stride > 2:
         rows = total.shape[0] // 2

time: 111 us -> 114 us (1.027)
  local copies, waits for them, and re-layouts: 8.26 us -> 15.2 us
  starting transfers between devices: 41.5 us -> 39.5 us
  waiting for transfers between devices: 41.8 us -> 40.1 us
    unnamed x40 -> x62, local copies, waits for them, and re-layouts: 6.3 us -> 13.3 us
    ppermute x31 -> x30, starting transfers between devices: 20 us -> 18 us  [swap(): return lax.ppermute(value, axis, pairs)]
    ppermute x31 -> x30, waiting for transfers between devices: 26.6 us -> 25.8 us  [swap(): return lax.ppermute(value, axis, pairs)]
  transfers between devices with their start and end apart: 43 -> 42, of which waited for: 20 -> 16; matrix products, arithmetic and copies ran while one was open for 3% -> 3% of each run, Pallas kernels for 12% -> 12%
where the time goes in v1:
time: 114 us
  waiting for transfers between devices  40.1 us (35%)
  starting transfers between devices  39.5 us (35%)
  local copies, waits for them, and re-layouts  15.2 us (13%)
  Pallas kernels  14.7 us (13%)
  other arithmetic  3.06 us (3%)
    ppermute x30, waiting for transfers between devices, swap(): return lax.ppermute(value, axis, pairs)  25.8 us
    ppermute x12, starting transfers between devices, ring_step(): return lax.ppermute(value, ('ctx', 'zero'), pairs)  21.5 us
    ppermute x30, starting transfers between devices, swap(): return lax.ppermute(value, axis, pairs)  18 us
    ppermute x12, waiting for transfers between devices, ring_step(): return lax.ppermute(value, ('ctx', 'zero'), pairs)  14.4 us
    unnamed x62, local copies, waits for them, and re-layouts  13.3 us
    pallas_call x1, Pallas kernels, project(): pl.pallas_call(functools.partial(project_kernel, layout), out_shape=[jax....  5.49 us
    pallas_call x4, Pallas kernels, mix(): pl.pallas_call(functools.partial(mix_kernel, layout, (sides, [len(block)...  4.1 us
    pallas_call x1, Pallas kernels, attend(): pl.pallas_call(functools.partial(attend_kernel, groups), out_shape=[jax.S...  3.85 us
  transfers between devices with their start and end apart: 42, of which 16 were waited for; matrix products, arithmetic and copies ran while one was open for 3% of the time, Pallas kernels for 12%

profile of v1, /device:TPU:0, one launch (start us, length us, event | category | flops | bytes accessed | tf_op | source)
XLA Modules:
  0.0 113.7 jit_solution(10402490550923312547)
XLA Ops:
  0.5 0.8 dynamic-slice_convert_fusion
  1.3 0.7 collective-permute-done.2
  2.0 1.4 %multiply_convert_fusion.refs_6_ = bf16[512,768]{1,0:T(8,128)(2,1)S(1)} fusion(bf16[512,256]{1,0:T(8,128)(2,1)S(1)} %collective-permute-done.3, bf16[512,256]{1,0:T(8,128)(2,1)} %param.10, bf16[512,128]{1,0:T(8,128)(2,1)S(1)} %collective-permute-done.2, bf16[512,128]{1,0:T(8,128)(2,1)} %bitcast.11, f32[512]{0:T(512)S(1)} %dynamic-slice_convert_fusion, pred[]{:T(512)S(6)} %eq.17), kind=kLoop, calls=%fused_computation | loop fusion | flops 7864320 | bytes 1574913 | tf_op jit(solution)/shard_map/convert_element_type | solution.py:457
  3.4 3.0 %collective-permute-start.4 = (bf16[256,768]{1,0:T(8,128)(2,1)S(1)}, bf16[256,768]{1,0:T(8,128)(2,1)S(1)}, u32[]{:S(2)}, u32[]{:S(2)}) collective-permute-start(bf16[256,768]{1,0:T(8,128)(2,1)S(1)} %get-tuple-element.44), channel_id=1, source_target_pairs={{0,8},{1,5},{2,10},{3,7},{8,16},{9,1},{10,18},{11,3},{16,24},{17,9... | collective-permute-start | bytes 1179656 | tf_op jit(solution)/shard_map/ppermute | solution.py:35
  6.4 1.6 %collective-permute-start.13 = (bf16[256,768]{1,0:T(8,128)(2,1)S(1)}, bf16[256,768]{1,0:T(8,128)(2,1)S(1)}, u32[]{:S(2)}, u32[]{:S(2)}) collective-permute-start(bf16[256,768]{1,0:T(8,128)(2,1)S(1)} %get-tuple-element.43), channel_id=1, source_target_pairs={{0,8},{1,5},{2,10},{3,7},{8,16},{9,1},{10,18},{11,3},{16,24},{17,9... | collective-permute-start | bytes 1179656 | tf_op jit(solution)/shard_map/ppermute | solution.py:35
  8.0 1.5 %collective-permute-start.1 = (bf16[512,1024]{1,0:T(8,128)(2,1)S(1)}, bf16[512,1024]{1,0:T(8,128)(2,1)S(1)}, u32[]{:S(2)}, u32[]{:S(2)}) collective-permute-start(bf16[512,1024]{1,0:T(8,128)(2,1)S(1)} %copy-done), channel_id=1, source_target_pairs={{0,2},{1,3},{2,0},{3,1},{4,6},{5,7},{6,4},{7,5},{8,10},{9,11},{10,... | collective-permute-start | bytes 3145736 | tf_op jit(solution)/shard_map/ppermute | solution.py:20
  9.5 2.6 %collective-permute-done.4.refs_7_ = bf16[256,768]{1,0:T(8,128)(2,1)S(1)} collective-permute-done((bf16[256,768]{1,0:T(8,128)(2,1)S(1)}, bf16[256,768]{1,0:T(8,128)(2,1)S(1)}, u32[]{:S(2)}, u32[]{:S(2)}) %collective-permute-start.4) | collective-permute-done | bytes 393248 | tf_op jit(solution)/shard_map/ppermute | solution.py:35
  12.1 2.1 %collective-permute-start.5 = (bf16[256,768]{1,0:T(8,128)(2,1)S(1)}, bf16[256,768]{1,0:T(8,128)(2,1)}, u32[]{:S(2)}, u32[]{:S(2)}) collective-permute-start(bf16[256,768]{1,0:T(8,128)(2,1)S(1)} %collective-permute-done.4.refs_7_), channel_id=1, source_target_pairs={{0,8},{1,5},{2,10},{3,7},{8,16},{9,1},{10,18},{11,3},{16,24},{17,9... | collective-permute-start | bytes 1179656 | tf_op jit(solution)/shard_map/ppermute | solution.py:35
  14.2 2.1 %collective-permute-done.13.refs_15_ = bf16[256,768]{1,0:T(8,128)(2,1)S(1)} collective-permute-done((bf16[256,768]{1,0:T(8,128)(2,1)S(1)}, bf16[256,768]{1,0:T(8,128)(2,1)S(1)}, u32[]{:S(2)}, u32[]{:S(2)}) %collective-permute-start.13) | collective-permute-done | bytes 393248 | tf_op jit(solution)/shard_map/ppermute | solution.py:35
  16.3 2.1 %collective-permute-start.15 = (bf16[256,768]{1,0:T(8,128)(2,1)S(1)}, bf16[256,768]{1,0:T(8,128)(2,1)}, u32[]{:S(2)}, u32[]{:S(2)}) collective-permute-start(bf16[256,768]{1,0:T(8,128)(2,1)S(1)} %collective-permute-done.13.refs_15_), channel_id=1, source_target_pairs={{0,8},{1,5},{2,10},{3,7},{8,16},{9,1},{10,18},{11,3},{16,24},{17,9... | collective-permute-start | bytes 1179656 | tf_op jit(solution)/shard_map/ppermute | solution.py:35
  18.4 0.7 copy-done.7
  19.2 1.5 %collective-permute-done.5.refs_9_ = bf16[256,768]{1,0:T(8,128)(2,1)} collective-permute-done((bf16[256,768]{1,0:T(8,128)(2,1)S(1)}, bf16[256,768]{1,0:T(8,128)(2,1)}, u32[]{:S(2)}, u32[]{:S(2)}) %collective-permute-start.5) | collective-permute-done | bytes 393248 | tf_op jit(solution)/shard_map/ppermute | solution.py:35
  20.6 0.8 copy-done.9
  21.4 2.1 %collective-permute-start.7 = (bf16[256,768]{1,0:T(8,128)(2,1)}, bf16[256,768]{1,0:T(8,128)(2,1)}, u32[]{:S(2)}, u32[]{:S(2)}) collective-permute-start(bf16[256,768]{1,0:T(8,128)(2,1)} %collective-permute-done.5.refs_9_), channel_id=1, source_target_pairs={{0,8},{1,5},{2,10},{3,7},{8,16},{9,1},{10,18},{11,3},{16,24},{17,9... | collective-permute-start | bytes 1179656 | tf_op jit(solution)/shard_map/ppermute | solution.py:35
  23.5 0.8 copy-done.11
  24.9 2.1 %collective-permute-start.17 = (bf16[256,768]{1,0:T(8,128)(2,1)}, bf16[256,768]{1,0:T(8,128)(2,1)}, u32[]{:S(2)}, u32[]{:S(2)}) collective-permute-start(bf16[256,768]{1,0:T(8,128)(2,1)} %collective-permute-done.15.refs_17_), channel_id=1, source_target_pairs={{0,8},{1,5},{2,10},{3,7},{8,16},{9,1},{10,18},{11,3},{16,24},{17,9... | collective-permute-start | bytes 1179656 | tf_op jit(solution)/shard_map/ppermute | solution.py:35
  27.0 2.5 %collective-permute-done.7.refs_11_ = bf16[256,768]{1,0:T(8,128)(2,1)} collective-permute-done((bf16[256,768]{1,0:T(8,128)(2,1)}, bf16[256,768]{1,0:T(8,128)(2,1)}, u32[]{:S(2)}, u32[]{:S(2)}) %collective-permute-start.7) | collective-permute-done | bytes 393248 | tf_op jit(solution)/shard_map/ppermute | solution.py:35
  29.5 0.9 constant_dynamic-slice_fusion.2
  30.5 2.2 %collective-permute-start.9 = (bf16[128,768]{1,0:T(8,128)(2,1)S(1)}, bf16[128,768]{1,0:T(8,128)(2,1)S(1)}, u32[]{:S(2)}, u32[]{:S(2)}) collective-permute-start(bf16[128,768]{1,0:T(8,128)(2,1)S(1)} %constant_dynamic-slice_fusion.2), channel_id=1, source_target_pairs={{0,8},{1,5},{2,10},{3,7},{8,16},{9,1},{10,18},{11,3},{16,24},{17,9... | collective-permute-start | bytes 589832 | tf_op jit(solution)/shard_map/ppermute | solution.py:35
  33.3 1.5 %collective-permute-start.23 = (bf16[256,512]{1,0:T(8,128)(2,1)}, bf16[256,512]{1,0:T(8,128)(2,1)S(1)}, u32[]{:S(2)}, u32[]{:S(2)}) collective-permute-start(bf16[256,512]{1,0:T(8,128)(2,1)} %param.12), channel_id=1, source_target_pairs={{0,2},{1,3},{2,0},{3,1},{4,6},{5,7},{6,4},{7,5},{8,10},{9,11},{10,... | collective-permute-start | bytes 786440 | tf_op jit(solution)/shard_map/ppermute | solution.py:20
  34.8 0.9 constant_dynamic-slice_fusion.1
  36.2 2.1 %collective-permute-start.19 = (bf16[128,768]{1,0:T(8,128)(2,1)S(1)}, bf16[128,768]{1,0:T(8,128)(2,1)S(1)}, u32[]{:S(2)}, u32[]{:S(2)}) collective-permute-start(bf16[128,768]{1,0:T(8,128)(2,1)S(1)} %constant_dynamic-slice_fusion.1), channel_id=1, source_target_pairs={{0,8},{1,5},{2,10},{3,7},{8,16},{9,1},{10,18},{11,3},{16,24},{17,9... | collective-permute-start | bytes 589832 | tf_op jit(solution)/shard_map/ppermute | solution.py:35
  38.7 3.1 %collective-permute-done.23.refs_3_ = bf16[256,512]{1,0:T(8,128)(2,1)S(1)} collective-permute-done((bf16[256,512]{1,0:T(8,128)(2,1)}, bf16[256,512]{1,0:T(8,128)(2,1)S(1)}, u32[]{:S(2)}, u32[]{:S(2)}) %collective-permute-start.23) | collective-permute-done | bytes 262176 | tf_op jit(solution)/shard_map/ppermute | solution.py:20
  42.5 1.6 %collective-permute-start.24 = (bf16[512,512]{1,0:T(8,128)(2,1)S(1)}, bf16[512,512]{1,0:T(8,128)(2,1)S(1)}, u32[]{:S(2)}, u32[]{:S(2)}) collective-permute-start(bf16[512,512]{1,0:T(8,128)(2,1)S(1)} %maximum_select_fusion.1.refs_2_), channel_id=1, source_target_pairs={{0,8},{1,5},{2,10},{3,7},{8,16},{9,1},{10,18},{11,3},{16,24},{17,9... | collective-permute-start | bytes 1572872 | tf_op jit(solution)/shard_map/ppermute | solution.py:35
  45.9 5.5 %shard_map.84 = (bf16[256,256]{1,0:T(8,128)(2,1)S(1)}, bf16[256,512]{1,0:T(8,128)(2,1)S(1)}) custom-call(f32[256,128]{1,0:T(8,128)S(1)} %get-tuple-element.48.refs_0_, f32[256,128]{1,0:T(8,128)S(1)} %get-tuple-element.49.refs_1_, bf16[512,1024]{1,0:T(8,128)(2,1)S(1)} %copy-done, bf16[256,1024]{1,0:T(8,128)(2,1)S(1)} %collective-permute-done.refs_3_, ...), custom_call_target="tpu_custom_call" | custom-call | flops 1610612736 | bytes 8388608 | tf_op jit(solution)/shard_map/pallas_call | solution.py:195
  52.2 0.8 copy-done.1
  53.0 0.9 collective-permute-start.25
  54.6 4.0 %collective-permute-done.25 = bf16[256,256]{1,0:T(8,128)(2,1)S(1)} collective-permute-done((bf16[256,256]{1,0:T(8,128)(2,1)S(1)}, bf16[256,256]{1,0:T(8,128)(2,1)S(1)}, u32[]{:S(2)}, u32[]{:S(2)}) %collective-permute-start.25) | collective-permute-done | bytes 131104 | tf_op jit(solution)/shard_map/ppermute | solution.py:20
  59.9 1.6 %collective-permute-start.26 = (bf16[256,256]{1,0:T(8,128)(2,1)S(1)}, bf16[256,256]{1,0:T(8,128)(2,1)S(1)}, u32[]{:S(2)}, u32[]{:S(2)}) collective-permute-start(bf16[256,256]{1,0:T(8,128)(2,1)S(1)} %broadcast_select_fusion), channel_id=1, source_target_pairs={{0,8},{4,12},{8,0},{12,4},{16,24},{20,28},{24,16},{28,20},{1,9},{5... | collective-permute-start | bytes 393224 | tf_op jit(solution)/shard_map/ppermute | solution.py:20
  61.5 1.5 %collective-permute-start.33 = (bf16[512,512]{1,0:T(8,128)(2,1)}, bf16[512,512]{1,0:T(8,128)(2,1)S(1)}, u32[]{:S(2)}, u32[]{:S(2)}) collective-permute-start(bf16[512,512]{1,0:T(8,128)(2,1)} %copy-done.1), channel_id=1, source_target_pairs={{0,2},{1,3},{2,0},{3,1},{4,6},{5,7},{6,4},{7,5},{8,10},{9,11},{10,... | collective-permute-start | bytes 1572872 | tf_op jit(solution)/shard_map/ppermute | solution.py:20
  63.5 1.4 %collective-permute-done.26 = bf16[256,256]{1,0:T(8,128)(2,1)S(1)} collective-permute-done((bf16[256,256]{1,0:T(8,128)(2,1)S(1)}, bf16[256,256]{1,0:T(8,128)(2,1)S(1)}, u32[]{:S(2)}, u32[]{:S(2)}) %collective-permute-start.26) | collective-permute-done | bytes 131104 | tf_op jit(solution)/shard_map/ppermute | solution.py:20
  64.9 2.6 %collective-permute-start.27 = (bf16[256,256]{1,0:T(8,128)(2,1)S(1)}, bf16[256,256]{1,0:T(8,128)(2,1)S(1)}, u32[]{:S(2)}, u32[]{:S(2)}) collective-permute-start(bf16[256,256]{1,0:T(8,128)(2,1)S(1)} %broadcast_select_fusion.1), channel_id=1, source_target_pairs={{0,16},{4,20},{8,24},{12,28},{16,0},{20,4},{24,8},{28,12},{1,17},{... | collective-permute-start | bytes 393224 | tf_op jit(solution)/shard_map/ppermute | solution.py:20
  67.5 6.2 %collective-permute-done.27 = bf16[256,256]{1,0:T(8,128)(2,1)S(1)} collective-permute-done((bf16[256,256]{1,0:T(8,128)(2,1)S(1)}, bf16[256,256]{1,0:T(8,128)(2,1)S(1)}, u32[]{:S(2)}, u32[]{:S(2)}) %collective-permute-start.27) | collective-permute-done | bytes 131104 | tf_op jit(solution)/shard_map/ppermute | solution.py:20
  73.8 4.4 %collective-permute-start.28 = (bf16[256,256]{1,0:T(8,128)(2,1)S(1)}, bf16[256,256]{1,0:T(8,128)(2,1)S(1)}, u32[]{:S(2)}, u32[]{:S(2)}) collective-permute-start(bf16[256,256]{1,0:T(8,128)(2,1)S(1)} %broadcast_select_fusion.2.refs_3_), channel_id=1, source_target_pairs={{0,1},{1,0},{2,3},{3,2},{4,5},{5,4},{6,7},{7,6},{8,9},{9,8},{10,11... | collective-permute-start | bytes 393224 | tf_op jit(solution)/shard_map/ppermute | solution.py:20
  78.8 0.8 copy-done.3
  80.3 1.0 collective-permute-start.36
  81.3 0.9 copy-done.19
  82.2 0.9 copy-done.21
  83.1 0.9 copy-done.23
  84.0 0.9 copy-done.25
  84.9 0.9 copy-done.27
  85.8 3.9 %shard_map.85 = (bf16[128,512]{1,0:T(8,128)(2,1)S(1)}, bf16[128,512]{1,0:T(8,128)(2,1)S(1)}) custom-call(s32[4,4]{1,0:T(4,128)S(1)} %bitcast.9, s32[4,4]{1,0:T(4,128)S(1)} %select_bitcast_fusion.far_ref, bf16[256,512]{1,0:T(8,128)(2,1)S(1)} %copy-done.23, bf16[256,256]{1,0:T(8,128)(2,1)S(1)} %copy-done.19, bf16[256,256]{1,0:T(8,128)(2,1)S(1)} %copy-done.25, ...), custom_call_target="tpu_custom_call" | custom-call | flops 268435456 | bytes 1048576 | tf_op jit(solution)/shard_map/pallas_call | solution.py:298
  91.2 1.2 %collective-permute-start.38 = (bf16[256,512]{1,0:T(8,128)(2,1)S(1)}, bf16[256,512]{1,0:T(8,128)(2,1)S(1)}, u32[]{:S(2)}, u32[]{:S(2)}) collective-permute-start(bf16[256,512]{1,0:T(8,128)(2,1)S(1)} %constant_dynamic-slice_fusion), channel_id=1, source_target_pairs={{0,8},{1,5},{2,10},{3,7},{8,16},{9,1},{10,18},{11,3},{16,24},{17,9... | collective-permute-start | bytes 786440 | tf_op jit(solution)/shard_map/ppermute | solution.py:35
  92.9 4.7 %collective-permute-done.38.refs_13_.refs_1_ = bf16[256,512]{1,0:T(8,128)(2,1)S(1)} collective-permute-done((bf16[256,512]{1,0:T(8,128)(2,1)S(1)}, bf16[256,512]{1,0:T(8,128)(2,1)S(1)}, u32[]{:S(2)}, u32[]{:S(2)}) %collective-permute-start.38) | collective-permute-done | bytes 262176 | tf_op jit(solution)/shard_map/ppermute | solution.py:35
  99.3 5.3 %collective-permute-done.31.refs_1_.refs_0_ = bf16[128,1536]{1,0:T(8,128)(2,1)S(1)} collective-permute-done((bf16[128,1536]{1,0:T(8,128)(2,1)}, bf16[128,1536]{1,0:T(8,128)(2,1)S(1)}, u32[]{:S(2)}, u32[]{:S(2)}) %collective-permute-start.31) | collective-permute-done | bytes 393248 | tf_op jit(solution)/shard_map/ppermute | solution.py:20
  105.5 2.7 %shard_map.87 = (f32[128,1536]{1,0:T(8,128)S(1)}, f32[128,2560]{1,0:T(8,128)S(1)}) custom-call(bf16[128,512]{1,0:T(8,128)(2,1)S(1)} %copy-done.17, bf16[128,1536]{1,0:T(8,128)(2,1)S(1)} %collective-permute-done.31.refs_1_.refs_0_, bf16[512,512]{1,0:T(8,128)(2,1)S(1)} %maximum_select_fusion.1.refs_2_, bf16[256,512]{1,0:T(8,128)(2,1)S(1)} %copy-done.15, ...), custom_call_target="tpu_custom_call" | custom-call | flops 872415232 | bytes 22544384 | tf_op jit(solution)/shard_map/pallas_call | solution.py:358
  108.1 4.4 %collective-permute-done.41.refs_2_ = bf16[128,512]{1,0:T(8,128)(2,1)S(1)} collective-permute-done((bf16[128,512]{1,0:T(8,128)(2,1)S(1)}, bf16[128,512]{1,0:T(8,128)(2,1)S(1)}, u32[]{:S(2)}, u32[]{:S(2)}) %collective-permute-start.41) | collective-permute-done | bytes 131104 | tf_op jit(solution)/shard_map/ppermute | solution.py:20
  112.6 1.2 %shard_map.90 = bf16[128,4096]{1,0:T(8,128)(2,1)} custom-call(f32[128,1536]{1,0:T(8,128)S(1)} %get-tuple-element.40.full_ref, f32[128,2560]{1,0:T(8,128)S(1)} %get-tuple-element.41.keep_ref, bf16[128,1536]{1,0:T(8,128)(2,1)S(1)} %collective-permute-done.31.refs_1_.refs_0_, bf16[128,1024]{1,0:T(8,128)(2,1)S(1)} %collective-permute-done.40.refs_1_, ...), custom_call_target="tpu_custom_call" | custom-call | flops 524288 | bytes 4194304 | tf_op jit(solution)/shard_map/pallas_call | solution.py:404
  (122 shorter events, 13.6 us)
Async XLA Ops:
  0.0 2.0 %collective-permute-start.3 = (bf16[512,256]{1,0:T(8,128)(2,1)}, bf16[512,256]{1,0:T(8,128)(2,1)S(1)}, u32[]{:S(2)}, u32[]{:S(2)}) collective-permute-start(bf16[512,256]{1,0:T(8,128)(2,1)} %param.10), channel_id=1, source_target_pairs={{0,1},{1,0},{2,3},{3,2},{4,5},{5,4},{6,7},{7,6},{8,9},{9,8},{10,11... | collective-permute-start | bytes 786440 | tf_op jit(solution)/shard_map/ppermute | solution.py:20
  0.5 1.6 %collective-permute-start.2 = (bf16[512,128]{1,0:T(8,128)(2,1)}, bf16[512,128]{1,0:T(8,128)(2,1)S(1)}, u32[]{:S(2)}, u32[]{:S(2)}) collective-permute-start(bf16[512,128]{1,0:T(8,128)(2,1)} %bitcast.10), channel_id=1, source_target_pairs={{0,1},{1,0},{2,3},{3,2},{4,5},{5,4},{6,7},{7,6},{8,9},{9,8},{10,11... | collective-permute-start | bytes 393224 | tf_op jit(solution)/shard_map/ppermute | solution.py:20
  3.4 8.7 %collective-permute-start.4 = (bf16[256,768]{1,0:T(8,128)(2,1)S(1)}, bf16[256,768]{1,0:T(8,128)(2,1)S(1)}, u32[]{:S(2)}, u32[]{:S(2)}) collective-permute-start(bf16[256,768]{1,0:T(8,128)(2,1)S(1)} %get-tuple-element.44), channel_id=1, source_target_pairs={{0,8},{1,5},{2,10},{3,7},{8,16},{9,1},{10,18},{11,3},{16,24},{17,9... | collective-permute-start | bytes 1179656 | tf_op jit(solution)/shard_map/ppermute | solution.py:35
  6.4 9.9 %collective-permute-start.13 = (bf16[256,768]{1,0:T(8,128)(2,1)S(1)}, bf16[256,768]{1,0:T(8,128)(2,1)S(1)}, u32[]{:S(2)}, u32[]{:S(2)}) collective-permute-start(bf16[256,768]{1,0:T(8,128)(2,1)S(1)} %get-tuple-element.43), channel_id=1, source_target_pairs={{0,8},{1,5},{2,10},{3,7},{8,16},{9,1},{10,18},{11,3},{16,24},{17,9... | collective-permute-start | bytes 1179656 | tf_op jit(solution)/shard_map/ppermute | solution.py:35
  8.0 24.7 %collective-permute-start.1 = (bf16[512,1024]{1,0:T(8,128)(2,1)S(1)}, bf16[512,1024]{1,0:T(8,128)(2,1)S(1)}, u32[]{:S(2)}, u32[]{:S(2)}) collective-permute-start(bf16[512,1024]{1,0:T(8,128)(2,1)S(1)} %copy-done), channel_id=1, source_target_pairs={{0,2},{1,3},{2,0},{3,1},{4,6},{5,7},{6,4},{7,5},{8,10},{9,11},{10,... | collective-permute-start | bytes 3145736 | tf_op jit(solution)/shard_map/ppermute | solution.py:20
  12.1 26.2 %copy-start.5 = (bf16[256,768]{1,0:T(8,128)(2,1)}, bf16[256,768]{1,0:T(8,128)(2,1)S(1)}, u32[]{:S(2)}) copy-start(bf16[256,768]{1,0:T(8,128)(2,1)S(1)} %collective-permute-done.4.refs_7_) | copy-start | bytes 1179652
  12.1 8.5 %collective-permute-start.5 = (bf16[256,768]{1,0:T(8,128)(2,1)S(1)}, bf16[256,768]{1,0:T(8,128)(2,1)}, u32[]{:S(2)}, u32[]{:S(2)}) collective-permute-start(bf16[256,768]{1,0:T(8,128)(2,1)S(1)} %collective-permute-done.4.refs_7_), channel_id=1, source_target_pairs={{0,8},{1,5},{2,10},{3,7},{8,16},{9,1},{10,18},{11,3},{16,24},{17,9... | collective-permute-start | bytes 1179656 | tf_op jit(solution)/shard_map/ppermute | solution.py:35
  14.2 6.4 %collective-permute-start.6 = (bf16[256,768]{1,0:T(8,128)(2,1)S(1)}, bf16[256,768]{1,0:T(8,128)(2,1)S(1)}, u32[]{:S(2)}, u32[]{:S(2)}) collective-permute-start(bf16[256,768]{1,0:T(8,128)(2,1)S(1)} %collective-permute-done.4.refs_7_), channel_id=1, source_target_pairs={{0,1},{1,0},{2,3},{3,2},{4,5},{5,4},{6,7},{7,6},{8,9},{9,8},{10,11... | collective-permute-start | bytes 1179656 | tf_op jit(solution)/shard_map/ppermute | solution.py:20
  16.3 7.2 %collective-permute-start.14 = (bf16[256,768]{1,0:T(8,128)(2,1)S(1)}, bf16[256,768]{1,0:T(8,128)(2,1)S(1)}, u32[]{:S(2)}, u32[]{:S(2)}) collective-permute-start(bf16[256,768]{1,0:T(8,128)(2,1)S(1)} %collective-permute-done.13.refs_15_), channel_id=1, source_target_pairs={{0,1},{1,0},{2,3},{3,2},{4,5},{5,4},{6,7},{7,6},{8,9},{9,8},{10,11... | collective-permute-start | bytes 1179656 | tf_op jit(solution)/shard_map/ppermute | solution.py:20
  16.3 8.5 %collective-permute-start.15 = (bf16[256,768]{1,0:T(8,128)(2,1)S(1)}, bf16[256,768]{1,0:T(8,128)(2,1)}, u32[]{:S(2)}, u32[]{:S(2)}) collective-permute-start(bf16[256,768]{1,0:T(8,128)(2,1)S(1)} %collective-permute-done.13.refs_15_), channel_id=1, source_target_pairs={{0,8},{1,5},{2,10},{3,7},{8,16},{9,1},{10,18},{11,3},{16,24},{17,9... | collective-permute-start | bytes 1179656 | tf_op jit(solution)/shard_map/ppermute | solution.py:35
  21.4 8.1 %collective-permute-start.7 = (bf16[256,768]{1,0:T(8,128)(2,1)}, bf16[256,768]{1,0:T(8,128)(2,1)}, u32[]{:S(2)}, u32[]{:S(2)}) collective-permute-start(bf16[256,768]{1,0:T(8,128)(2,1)} %collective-permute-done.5.refs_9_), channel_id=1, source_target_pairs={{0,8},{1,5},{2,10},{3,7},{8,16},{9,1},{10,18},{11,3},{16,24},{17,9... | collective-permute-start | bytes 1179656 | tf_op jit(solution)/shard_map/ppermute | solution.py:35
  23.5 6.9 %collective-permute-start.8 = (bf16[256,768]{1,0:T(8,128)(2,1)}, bf16[256,768]{1,0:T(8,128)(2,1)}, u32[]{:S(2)}, u32[]{:S(2)}) collective-permute-start(bf16[256,768]{1,0:T(8,128)(2,1)} %collective-permute-done.5.refs_9_), channel_id=1, source_target_pairs={{0,1},{1,0},{2,3},{3,2},{4,5},{5,4},{6,7},{7,6},{8,9},{9,8},{10,11... | collective-permute-start | bytes 1179656 | tf_op jit(solution)/shard_map/ppermute | solution.py:20
  24.9 8.4 %collective-permute-start.16 = (bf16[256,768]{1,0:T(8,128)(2,1)}, bf16[256,768]{1,0:T(8,128)(2,1)}, u32[]{:S(2)}, u32[]{:S(2)}) collective-permute-start(bf16[256,768]{1,0:T(8,128)(2,1)} %collective-permute-done.15.refs_17_), channel_id=1, source_target_pairs={{0,1},{1,0},{2,3},{3,2},{4,5},{5,4},{6,7},{7,6},{8,9},{9,8},{10,11... | collective-permute-start | bytes 1179656 | tf_op jit(solution)/shard_map/ppermute | solution.py:20
  24.9 9.9 %collective-permute-start.17 = (bf16[256,768]{1,0:T(8,128)(2,1)}, bf16[256,768]{1,0:T(8,128)(2,1)}, u32[]{:S(2)}, u32[]{:S(2)}) collective-permute-start(bf16[256,768]{1,0:T(8,128)(2,1)} %collective-permute-done.15.refs_17_), channel_id=1, source_target_pairs={{0,8},{1,5},{2,10},{3,7},{8,16},{9,1},{10,18},{11,3},{16,24},{17,9... | collective-permute-start | bytes 1179656 | tf_op jit(solution)/shard_map/ppermute | solution.py:35
  30.5 5.7 %collective-permute-start.9 = (bf16[128,768]{1,0:T(8,128)(2,1)S(1)}, bf16[128,768]{1,0:T(8,128)(2,1)S(1)}, u32[]{:S(2)}, u32[]{:S(2)}) collective-permute-start(bf16[128,768]{1,0:T(8,128)(2,1)S(1)} %constant_dynamic-slice_fusion.2), channel_id=1, source_target_pairs={{0,8},{1,5},{2,10},{3,7},{8,16},{9,1},{10,18},{11,3},{16,24},{17,9... | collective-permute-start | bytes 589832 | tf_op jit(solution)/shard_map/ppermute | solution.py:35
  32.7 11.4 %collective-permute-start = (bf16[256,1024]{1,0:T(8,128)(2,1)S(1)}, bf16[256,1024]{1,0:T(8,128)(2,1)S(1)}, u32[]{:S(2)}, u32[]{:S(2)}) collective-permute-start(bf16[256,1024]{1,0:T(8,128)(2,1)S(1)} %shard_map.82), channel_id=1, source_target_pairs={{0,1},{1,0},{2,3},{3,2},{4,5},{5,4},{6,7},{7,6},{8,9},{9,8},{10,11... | collective-permute-start | bytes 1572872 | tf_op jit(solution)/shard_map/ppermute | solution.py:20
  32.8 5.6 %collective-permute-start.22 = (bf16[256,512]{1,0:T(8,128)(2,1)}, bf16[256,512]{1,0:T(8,128)(2,1)S(1)}, u32[]{:S(2)}, u32[]{:S(2)}) collective-permute-start(bf16[256,512]{1,0:T(8,128)(2,1)} %param.12), channel_id=1, source_target_pairs={{0,1},{1,0},{2,3},{3,2},{4,5},{5,4},{6,7},{7,6},{8,9},{9,8},{10,11... | collective-permute-start | bytes 786440 | tf_op jit(solution)/shard_map/ppermute | solution.py:20
  33.3 8.5 %collective-permute-start.23 = (bf16[256,512]{1,0:T(8,128)(2,1)}, bf16[256,512]{1,0:T(8,128)(2,1)S(1)}, u32[]{:S(2)}, u32[]{:S(2)}) collective-permute-start(bf16[256,512]{1,0:T(8,128)(2,1)} %param.12), channel_id=1, source_target_pairs={{0,2},{1,3},{2,0},{3,1},{4,6},{5,7},{6,4},{7,5},{8,10},{9,11},{10,... | collective-permute-start | bytes 786440 | tf_op jit(solution)/shard_map/ppermute | solution.py:20
  34.8 9.4 %collective-permute-start.11 = (bf16[256,768]{1,0:T(8,128)(2,1)}, bf16[256,768]{1,0:T(8,128)(2,1)S(1)}, u32[]{:S(2)}, u32[]{:S(2)}) collective-permute-start(bf16[256,768]{1,0:T(8,128)(2,1)} %collective-permute-done.7.refs_11_), channel_id=1, source_target_pairs={{0,1},{1,0},{2,3},{3,2},{4,5},{5,4},{6,7},{7,6},{8,9},{9,8},{10,11... | collective-permute-start | bytes 1179656 | tf_op jit(solution)/shard_map/ppermute | solution.py:20
  36.2 6.3 %collective-permute-start.19 = (bf16[128,768]{1,0:T(8,128)(2,1)S(1)}, bf16[128,768]{1,0:T(8,128)(2,1)S(1)}, u32[]{:S(2)}, u32[]{:S(2)}) collective-permute-start(bf16[128,768]{1,0:T(8,128)(2,1)S(1)} %constant_dynamic-slice_fusion.1), channel_id=1, source_target_pairs={{0,8},{1,5},{2,10},{3,7},{8,16},{9,1},{10,18},{11,3},{16,24},{17,9... | collective-permute-start | bytes 589832 | tf_op jit(solution)/shard_map/ppermute | solution.py:35
  38.4 7.5 %collective-permute-start.10 = (bf16[256,1024]{1,0:T(8,128)(2,1)S(1)}, bf16[256,1024]{1,0:T(8,128)(2,1)S(1)}, u32[]{:S(2)}, u32[]{:S(2)}) collective-permute-start(bf16[256,1024]{1,0:T(8,128)(2,1)S(1)} %shard_map.83), channel_id=1, source_target_pairs={{0,1},{1,0},{2,3},{3,2},{4,5},{5,4},{6,7},{7,6},{8,9},{9,8},{10,11... | collective-permute-start | bytes 1572872 | tf_op jit(solution)/shard_map/ppermute | solution.py:20
  41.8 3.8 %collective-permute-start.18 = (bf16[256,768]{1,0:T(8,128)(2,1)}, bf16[256,768]{1,0:T(8,128)(2,1)S(1)}, u32[]{:S(2)}, u32[]{:S(2)}) collective-permute-start(bf16[256,768]{1,0:T(8,128)(2,1)} %collective-permute-done.17.refs_19_), channel_id=1, source_target_pairs={{0,1},{1,0},{2,3},{3,2},{4,5},{5,4},{6,7},{7,6},{8,9},{9,8},{10,11... | collective-permute-start | bytes 1179656 | tf_op jit(solution)/shard_map/ppermute | solution.py:20
  42.5 9.7 %collective-permute-start.24 = (bf16[512,512]{1,0:T(8,128)(2,1)S(1)}, bf16[512,512]{1,0:T(8,128)(2,1)S(1)}, u32[]{:S(2)}, u32[]{:S(2)}) collective-permute-start(bf16[512,512]{1,0:T(8,128)(2,1)S(1)} %maximum_select_fusion.1.refs_2_), channel_id=1, source_target_pairs={{0,8},{1,5},{2,10},{3,7},{8,16},{9,1},{10,18},{11,3},{16,24},{17,9... | collective-permute-start | bytes 1572872 | tf_op jit(solution)/shard_map/ppermute | solution.py:35
  44.1 1.5 %collective-permute-start.12 = (bf16[128,768]{1,0:T(8,128)(2,1)S(1)}, bf16[128,768]{1,0:T(8,128)(2,1)S(1)}, u32[]{:S(2)}, u32[]{:S(2)}) collective-permute-start(bf16[128,768]{1,0:T(8,128)(2,1)S(1)} %collective-permute-done.9.refs_13_), channel_id=1, source_target_pairs={{0,1},{1,0},{2,3},{3,2},{4,5},{5,4},{6,7},{7,6},{8,9},{9,8},{10,11... | collective-permute-start | bytes 589832 | tf_op jit(solution)/shard_map/ppermute | solution.py:20
  44.2 1.7 %collective-permute-start.20 = (bf16[128,768]{1,0:T(8,128)(2,1)S(1)}, bf16[128,768]{1,0:T(8,128)(2,1)S(1)}, u32[]{:S(2)}, u32[]{:S(2)}) collective-permute-start(bf16[128,768]{1,0:T(8,128)(2,1)S(1)} %collective-permute-done.19.refs_21_), channel_id=1, source_target_pairs={{0,1},{1,0},{2,3},{3,2},{4,5},{5,4},{6,7},{7,6},{8,9},{9,8},{10,11... | collective-permute-start | bytes 589832 | tf_op jit(solution)/shard_map/ppermute | solution.py:20
  45.9 35.3 %copy-start.30 = (s32[1,4,4]{2,1,0:T(4,128)S(1)}, s32[1,4,4]{2,1,0:T(4,128)}, u32[]{:S(2)}) copy-start(s32[1,4,4]{2,1,0:T(4,128)} %param.14) | copy-start | bytes 196
  45.9 35.3 %copy-start.28 = (s32[1,4,4]{2,1,0:T(4,128)S(1)}, s32[1,4,4]{2,1,0:T(4,128)}, u32[]{:S(2)}) copy-start(s32[1,4,4]{2,1,0:T(4,128)} %param.13) | copy-start | bytes 196
  53.0 5.6 %collective-permute-start.25 = (bf16[256,256]{1,0:T(8,128)(2,1)S(1)}, bf16[256,256]{1,0:T(8,128)(2,1)S(1)}, u32[]{:S(2)}, u32[]{:S(2)}) collective-permute-start(bf16[256,256]{1,0:T(8,128)(2,1)S(1)} %get-tuple-element.32.refs_1_), channel_id=1, source_target_pairs={{0,4},{4,0},{8,12},{12,8},{16,20},{20,16},{24,28},{28,24},{1,5},{5... | collective-permute-start | bytes 393224 | tf_op jit(solution)/shard_map/ppermute | solution.py:20
  54.5 4.8 %collective-permute-start.21 = (bf16[256,256]{1,0:T(8,128)(2,1)S(1)}, bf16[256,256]{1,0:T(8,128)(2,1)S(1)}, u32[]{:S(2)}, u32[]{:S(2)}) collective-permute-start(bf16[256,256]{1,0:T(8,128)(2,1)S(1)} %get-tuple-element.32.refs_1_), channel_id=1, source_target_pairs={{0,1},{1,0},{2,3},{3,2},{4,5},{5,4},{6,7},{7,6},{8,9},{9,8},{10,11... | collective-permute-start | bytes 393224 | tf_op jit(solution)/shard_map/ppermute | solution.py:20
  59.9 5.0 %collective-permute-start.26 = (bf16[256,256]{1,0:T(8,128)(2,1)S(1)}, bf16[256,256]{1,0:T(8,128)(2,1)S(1)}, u32[]{:S(2)}, u32[]{:S(2)}) collective-permute-start(bf16[256,256]{1,0:T(8,128)(2,1)S(1)} %broadcast_select_fusion), channel_id=1, source_target_pairs={{0,8},{4,12},{8,0},{12,4},{16,24},{20,28},{24,16},{28,20},{1,9},{5... | collective-permute-start | bytes 393224 | tf_op jit(solution)/shard_map/ppermute | solution.py:20
  61.5 17.3 %collective-permute-start.33 = (bf16[512,512]{1,0:T(8,128)(2,1)}, bf16[512,512]{1,0:T(8,128)(2,1)S(1)}, u32[]{:S(2)}, u32[]{:S(2)}) collective-permute-start(bf16[512,512]{1,0:T(8,128)(2,1)} %copy-done.1), channel_id=1, source_target_pairs={{0,2},{1,3},{2,0},{3,1},{4,6},{5,7},{6,4},{7,5},{8,10},{9,11},{10,... | collective-permute-start | bytes 1572872 | tf_op jit(solution)/shard_map/ppermute | solution.py:20
  63.0 15.8 %collective-permute-start.34 = (bf16[512,512]{1,0:T(8,128)(2,1)}, bf16[512,512]{1,0:T(8,128)(2,1)S(1)}, u32[]{:S(2)}, u32[]{:S(2)}) collective-permute-start(bf16[512,512]{1,0:T(8,128)(2,1)} %copy-done.1), channel_id=1, source_target_pairs={{0,1},{1,0},{2,3},{3,2},{4,5},{5,4},{6,7},{7,6},{8,9},{9,8},{10,11... | collective-permute-start | bytes 1572872 | tf_op jit(solution)/shard_map/ppermute | solution.py:20
  63.0 15.7 %collective-permute-start.29 = (bf16[512,512]{1,0:T(8,128)(2,1)}, bf16[512,512]{1,0:T(8,128)(2,1)S(1)}, u32[]{:S(2)}, u32[]{:S(2)}) collective-permute-start(bf16[512,512]{1,0:T(8,128)(2,1)} %copy-done.1), channel_id=1, source_target_pairs={{0,8},{1,5},{2,10},{3,7},{8,16},{9,1},{10,18},{11,3},{16,24},{17,9... | collective-permute-start | bytes 1572872 | tf_op jit(solution)/shard_map/ppermute | solution.py:35
  64.9 8.8 %collective-permute-start.27 = (bf16[256,256]{1,0:T(8,128)(2,1)S(1)}, bf16[256,256]{1,0:T(8,128)(2,1)S(1)}, u32[]{:S(2)}, u32[]{:S(2)}) collective-permute-start(bf16[256,256]{1,0:T(8,128)(2,1)S(1)} %broadcast_select_fusion.1), channel_id=1, source_target_pairs={{0,16},{4,20},{8,24},{12,28},{16,0},{20,4},{24,8},{28,12},{1,17},{... | collective-permute-start | bytes 393224 | tf_op jit(solution)/shard_map/ppermute | solution.py:20
  73.8 5.9 %collective-permute-start.28 = (bf16[256,256]{1,0:T(8,128)(2,1)S(1)}, bf16[256,256]{1,0:T(8,128)(2,1)S(1)}, u32[]{:S(2)}, u32[]{:S(2)}) collective-permute-start(bf16[256,256]{1,0:T(8,128)(2,1)S(1)} %broadcast_select_fusion.2.refs_3_), channel_id=1, source_target_pairs={{0,1},{1,0},{2,3},{3,2},{4,5},{5,4},{6,7},{7,6},{8,9},{9,8},{10,11... | collective-permute-start | bytes 393224 | tf_op jit(solution)/shard_map/ppermute | solution.py:20
  78.8 10.9 %collective-permute-start.30 = (bf16[512,512]{1,0:T(8,128)(2,1)S(1)}, bf16[512,512]{1,0:T(8,128)(2,1)S(1)}, u32[]{:S(2)}, u32[]{:S(2)}) collective-permute-start(bf16[512,512]{1,0:T(8,128)(2,1)S(1)} %collective-permute-done.29.refs_1_.refs_9_), channel_id=1, source_target_pairs={{0,1},{1,0},{2,3},{3,2},{4,5},{5,4},{6,7},{7,6},{8,9},{9,8},{10,11... | collective-permute-start | bytes 1572872 | tf_op jit(solution)/shard_map/ppermute | solution.py:20
  80.3 10.8 %collective-permute-start.36 = (bf16[512,512]{1,0:T(8,128)(2,1)S(1)}, bf16[512,512]{1,0:T(8,128)(2,1)S(1)}, u32[]{:S(2)}, u32[]{:S(2)}) collective-permute-start(bf16[512,512]{1,0:T(8,128)(2,1)S(1)} %collective-permute-done.29.refs_1_.refs_9_), channel_id=1, source_target_pairs={{0,8},{1,5},{2,10},{3,7},{8,16},{9,1},{10,18},{11,3},{16,24},{17,9... | collective-permute-start | bytes 1572872 | tf_op jit(solution)/shard_map/ppermute | solution.py:35
  91.0 7.1 %collective-permute-start.37 = (bf16[512,512]{1,0:T(8,128)(2,1)S(1)}, bf16[512,512]{1,0:T(8,128)(2,1)S(1)}, u32[]{:S(2)}, u32[]{:S(2)}) collective-permute-start(bf16[512,512]{1,0:T(8,128)(2,1)S(1)} %collective-permute-done.36.refs_11_.refs_1_), channel_id=1, source_target_pairs={{0,1},{1,0},{2,3},{3,2},{4,5},{5,4},{6,7},{7,6},{8,9},{9,8},{10,11... | collective-permute-start | bytes 1572872 | tf_op jit(solution)/shard_map/ppermute | solution.py:20
  91.1 14.3 %copy-start.2 = (bf16[512,512]{1,0:T(8,128)(2,1)S(1)}, bf16[512,512]{1,0:T(8,128)(2,1)}, u32[]{:S(2)}) copy-start(bf16[512,512]{1,0:T(8,128)(2,1)} %copy-done.1) | copy-start | bytes 1572868
  91.2 14.3 %copy-start.4 = (bf16[512,512]{1,0:T(8,128)(2,1)S(1)}, bf16[512,512]{1,0:T(8,128)(2,1)}, u32[]{:S(2)}) copy-start(bf16[512,512]{1,0:T(8,128)(2,1)} %copy-done.3) | copy-start | bytes 1572868
  91.2 14.3 %copy-start.17 = (bf16[128,512]{1,0:T(8,128)(2,1)S(1)}, bf16[128,512]{1,0:T(8,128)(2,1)}, u32[]{:S(2)}) copy-start(bf16[128,512]{1,0:T(8,128)(2,1)} %copy-done.16) | copy-start | bytes 393220
  91.2 6.4 %collective-permute-start.38 = (bf16[256,512]{1,0:T(8,128)(2,1)S(1)}, bf16[256,512]{1,0:T(8,128)(2,1)S(1)}, u32[]{:S(2)}, u32[]{:S(2)}) collective-permute-start(bf16[256,512]{1,0:T(8,128)(2,1)S(1)} %constant_dynamic-slice_fusion), channel_id=1, source_target_pairs={{0,8},{1,5},{2,10},{3,7},{8,16},{9,1},{10,18},{11,3},{16,24},{17,9... | collective-permute-start | bytes 786440 | tf_op jit(solution)/shard_map/ppermute | solution.py:35
  92.4 13.0 %collective-permute-start.35 = (bf16[512,512]{1,0:T(8,128)(2,1)S(1)}, bf16[512,512]{1,0:T(8,128)(2,1)S(1)}, u32[]{:S(2)}, u32[]{:S(2)}) collective-permute-start(bf16[512,512]{1,0:T(8,128)(2,1)S(1)} %collective-permute-done.33.refs_6_), channel_id=1, source_target_pairs={{0,1},{1,0},{2,3},{3,2},{4,5},{5,4},{6,7},{7,6},{8,9},{9,8},{10,11... | collective-permute-start | bytes 1572872 | tf_op jit(solution)/shard_map/ppermute | solution.py:20
  92.4 12.1 %collective-permute-start.31 = (bf16[128,1536]{1,0:T(8,128)(2,1)}, bf16[128,1536]{1,0:T(8,128)(2,1)S(1)}, u32[]{:S(2)}, u32[]{:S(2)}) collective-permute-start(bf16[128,1536]{1,0:T(8,128)(2,1)} %copy-done.13), channel_id=1, source_target_pairs={{0,2},{1,3},{2,0},{3,1},{4,6},{5,7},{6,4},{7,5},{8,10},{9,11},{10,... | collective-permute-start | bytes 1179656 | tf_op jit(solution)/shard_map/ppermute | solution.py:20
  97.6 6.9 %collective-permute-start.39 = (bf16[256,512]{1,0:T(8,128)(2,1)S(1)}, bf16[256,512]{1,0:T(8,128)(2,1)S(1)}, u32[]{:S(2)}, u32[]{:S(2)}) collective-permute-start(bf16[256,512]{1,0:T(8,128)(2,1)S(1)} %collective-permute-done.38.refs_13_.refs_1_), channel_id=1, source_target_pairs={{0,1},{1,0},{2,3},{3,2},{4,5},{5,4},{6,7},{7,6},{8,9},{9,8},{10,11... | collective-permute-start | bytes 786440 | tf_op jit(solution)/shard_map/ppermute | solution.py:20
  97.6 7.8 %collective-permute-start.32 = (bf16[256,512]{1,0:T(8,128)(2,1)S(1)}, bf16[256,512]{1,0:T(8,128)(2,1)S(1)}, u32[]{:S(2)}, u32[]{:S(2)}) collective-permute-start(bf16[256,512]{1,0:T(8,128)(2,1)S(1)} %copy-done.15), channel_id=1, source_target_pairs={{0,1},{1,0},{2,3},{3,2},{4,5},{5,4},{6,7},{7,6},{8,9},{9,8},{10,11... | collective-permute-start | bytes 786440 | tf_op jit(solution)/shard_map/ppermute | solution.py:20
  98.7 13.9 %collective-permute-start.40 = (bf16[128,1024]{1,0:T(8,128)(2,1)S(1)}, bf16[128,1024]{1,0:T(8,128)(2,1)S(1)}, u32[]{:S(2)}, u32[]{:S(2)}) collective-permute-start(bf16[128,1024]{1,0:T(8,128)(2,1)S(1)} %shard_map.88), channel_id=1, source_target_pairs={{0,2},{1,3},{2,0},{3,1},{4,6},{5,7},{6,4},{7,5},{8,10},{9,11},{10,... | collective-permute-start | bytes 786440 | tf_op jit(solution)/shard_map/ppermute | solution.py:20
  104.8 7.7 %collective-permute-start.41 = (bf16[128,512]{1,0:T(8,128)(2,1)S(1)}, bf16[128,512]{1,0:T(8,128)(2,1)S(1)}, u32[]{:S(2)}, u32[]{:S(2)}) collective-permute-start(bf16[128,512]{1,0:T(8,128)(2,1)S(1)} %shard_map.89), channel_id=1, source_target_pairs={{0,2},{1,3},{2,0},{3,1},{4,6},{5,7},{6,4},{7,5},{8,10},{9,11},{10,... | collective-permute-start | bytes 393224 | tf_op jit(solution)/shard_map/ppermute | solution.py:20
  (25 other events, 69.1 us)
